TPU v7x, 128 devices: a whole 4x4x4 slice. The times are simulated.
128 devices in a mesh: group: 16 (over x, z), tensor: 8 (over y, core).
Axes of the slice: x: 4, y: 4, z: 4, core: 2. Of those that a mesh axis runs over, the one named last changes fastest.
Arguments:
- queries: bfloat16 [16384, 4096], P(('group', 'tensor')), may hold values from -6 to 6
- rotated_key_rows: bfloat16 [16384, 256], P(('group', 'tensor')), may hold values from -6 to 6
- value_row_matrix: bfloat16 [16384, 256], P(('group', 'tensor')), may hold values from -12 to 12
- out_weight: bfloat16 [4096, 4096], P('tensor'), may hold values from -0.09375 to 0.09375
- residual: bfloat16 [16384, 4096], P(('group', 'tensor')), may hold values from -3 to 3
- norm_gain: float32 [4096], replicated, may hold values from 0.25 to 1.75
- expert_ids: int32 [16384, 3], P(('group', 'tensor')), may hold values from 0 to 63, all different within a row; in each aligned block of 128 rows (0 to 127, 128 to 255, ...) at most 8 rows name the same one
- gate_weights: float32 [16384, 3], P(('group', 'tensor')), may hold values from 0.05 to 0.6
- w_gate: bfloat16 [128, 4096, 768], P(('group', 'tensor')), may hold values from -0.09375 to 0.09375
- w_up: bfloat16 [128, 4096, 768], P(('group', 'tensor')), may hold values from -0.09375 to 0.09375
- w_down: bfloat16 [128, 768, 4096], P(('group', 'tensor')), may hold values from -0.15625 to 0.15625
Outputs:
- mixed: bfloat16 [16384, 4096], P(('group', 'tensor'))
Inputs may be any that keep to these rules, and one draw needn't show every extreme that they name: `expert_ids`: the 3 experts of a row differ. Among the 128 rows of one device (aligned blocks), at most 8 name one expert, and in every draw some expert is named by exactly 8 of them.
All inputs are finite; a program needn't handle non-finite values.
Results may differ from a plain program's by a relative error of at most 0.0065.
Values may be sent and summed in bfloat16 or wider, within the bound.
No kernel may reach another device: no remote copies, remote signals or barrier semaphores. Data moves between devices by JAX's collectives and lax.ppermute only.
A program may use at most 128 MiB of HBM per device.

v0:
```python
import jax
import jax.numpy as jnp
from jax import lax
from jax.sharding import PartitionSpec as P

KEY_VALUE_HEADS = 2
HEAD_SIZE = 128
TOP = 3


def attend_rows(query_tile, key_tile, value_tile, first_row):
    row_total = query_tile.shape[0]
    column_count = key_tile.shape[0]
    kv_count = key_tile.shape[1]
    grouped_queries = query_tile.reshape(row_total, kv_count, -1, HEAD_SIZE)
    scores = jnp.einsum(
        "rkgd,ckd->kgrc", grouped_queries, key_tile, preferred_element_type=jnp.float32
    ) * HEAD_SIZE ** (-0.5)
    positions = first_row + jnp.arange(row_total, dtype=jnp.int32)
    allowed = jnp.arange(column_count, dtype=jnp.int32)[None, :] <= positions[:, None]
    scores = jnp.where(allowed, scores, -1e30)
    largest = jnp.max(scores, axis=-1, keepdims=True)
    weights = jnp.exp(scores - largest)
    probs = (weights / jnp.sum(weights, axis=-1, keepdims=True)).astype(jnp.bfloat16)
    context = jnp.einsum("kgrc,ckd->rkgd", probs, value_tile, preferred_element_type=jnp.float32)
    return context.astype(jnp.bfloat16).reshape(row_total, -1)


def local(
    queries,
    rotated_key_rows,
    value_row_matrix,
    out_weight,
    residual,
    norm_gain,
    expert_ids,
    gate_weights,
    w_gate,
    w_up,
    w_down,
):
    tensor_size = lax.axis_size("tensor")
    tensor_place = lax.axis_index("tensor")
    rows_here = queries.shape[0]
    span_row_slice = rows_here * tensor_size
    key_gathered, value_gathered = (
        lax.all_gather(rotated_key_rows, "tensor", axis=0, tiled=True),
        lax.all_gather(value_row_matrix, "tensor", axis=0, tiled=True),
    )
    own_context = attend_rows(
        queries,
        key_gathered.reshape(span_row_slice, KEY_VALUE_HEADS, HEAD_SIZE),
        value_gathered.reshape(span_row_slice, KEY_VALUE_HEADS, HEAD_SIZE),
        tensor_place * rows_here,
    )
    context = lax.all_to_all(own_context, "tensor", split_axis=1, concat_axis=0, tiled=True)
    projected = lax.psum_scatter(
        jnp.dot(context, out_weight, preferred_element_type=jnp.float32),
        "tensor",
        scatter_dimension=0,
        tiled=True,
    )
    hidden_state = residual.astype(jnp.float32) + projected
    mean_square = jnp.mean(hidden_state * hidden_state, axis=-1, keepdims=True)
    moe_input = (hidden_state * lax.rsqrt(mean_square + 1e-06) * norm_gain).astype(jnp.bfloat16)
    expert_count = lax.axis_size("group") * tensor_size // 2
    capacity = max(2, 2 * ((rows_here * TOP * 5 // (expert_count * 4) + 1) // 2))
    width = moe_input.shape[1]
    flat_ids = expert_ids.reshape(-1)
    one_hot = (flat_ids[:, None] == jnp.arange(expert_count, dtype=jnp.int32)[None, :]).astype(
        jnp.int32
    )
    earlier = jnp.cumsum(one_hot, axis=0) - one_hot
    rank_within = jnp.sum(earlier * one_hot, axis=1)
    slot_index = flat_ids * capacity + rank_within
    selector = jnp.arange(expert_count * capacity, dtype=jnp.int32)[:, None] == slot_index[None, :]
    selector = (
        selector.reshape(expert_count * capacity, rows_here, TOP).sum(axis=2).astype(jnp.bfloat16)
    )
    outgoing = jnp.dot(selector, moe_input, preferred_element_type=jnp.float32).astype(jnp.bfloat16)
    outgoing = outgoing.reshape(expert_count, capacity, width)
    doubled = jnp.broadcast_to(outgoing[:, None], (expert_count, 2, capacity, width)).reshape(
        2 * expert_count, capacity, width
    )
    slot_rows = lax.all_to_all(
        doubled, ("group", "tensor"), split_axis=0, concat_axis=0, tiled=True
    )
    sources, slots, _ = slot_rows.shape
    flat_rows = slot_rows.reshape(sources * slots, width)
    gate = jnp.dot(flat_rows, w_gate[0], preferred_element_type=jnp.float32)
    upward = jnp.dot(flat_rows, w_up[0], preferred_element_type=jnp.float32)
    activation = (jax.nn.silu(gate) * upward).astype(jnp.bfloat16)
    piece = jnp.dot(activation, w_down[0], preferred_element_type=jnp.float32).astype(jnp.bfloat16)
    pieces = piece.reshape(sources, slots, width)
    returned = lax.all_to_all(pieces, ("group", "tensor"), split_axis=0, concat_axis=0, tiled=True)
    returned = (
        lax.optimization_barrier(returned)
        .reshape(expert_count, 2, capacity, width)
        .astype(jnp.float32)
    )
    expert_out = (returned[:, 0] + returned[:, 1]).astype(jnp.bfloat16)
    expert_out = lax.optimization_barrier(expert_out)
    flat_out = expert_out.reshape(expert_count * capacity, width)
    picked = jnp.take(flat_out, slot_index, axis=0).reshape(rows_here, TOP, width)
    routed = jnp.sum(picked.astype(jnp.float32) * gate_weights[:, :, None], axis=1)
    return (hidden_state + routed).astype(jnp.bfloat16)


def solution(mesh):
    return jax.shard_map(
        local,
        mesh=mesh,
        in_specs=(
            P(("group", "tensor"), None),
            P(("group", "tensor"), None),
            P(("group", "tensor"), None),
            P("tensor", None),
            P(("group", "tensor"), None),
            P(),
            P(("group", "tensor"), None),
            P(("group", "tensor"), None),
            P(("group", "tensor"), None, None),
            P(("group", "tensor"), None, None),
            P(("group", "tensor"), None, None),
        ),
        out_specs=P(("group", "tensor"), None),
        check_vma=False,
    )
```

profile of v0, /device:TPU:1, one launch (start us, length us, event | category | flops | bytes accessed | tf_op | source)
XLA Modules:
  0.0 493.4 jit_solution(12778360010187241476)
XLA Ops:
  6.5 1.4 copy.70
  8.0 1.0 copy.47
  8.9 14.3 %all_gather.6 = bf16[1024,256]{0,1:T(8,128)(2,1)S(1)} all-gather(bf16[128,256]{0,1:T(8,128)(2,1)S(1)} %copy.47), channel_id=1, replica_groups=mesh['group'=16,'tensor'=8] {'tensor'}, dimensions={0}, use_global_device_ids=true | all-gather | bytes 589824 | tf_op jit(solution)/shard_map/all_gather | solution.py:47
  23.3 13.3 %all_gather.7 = bf16[1024,256]{1,0:T(8,128)(2,1)S(1)} all-gather(bf16[128,256]{1,0:T(8,128)(2,1)} %param.13), channel_id=1, replica_groups=mesh['group'=16,'tensor'=8] {'tensor'}, dimensions={0}, use_global_device_ids=true | all-gather | bytes 589824 | tf_op jit(solution)/shard_map/all_gather | solution.py:48
  36.9 9.0 %fusion.43 = (f32[2,16,128]{2,1,0:T(8,128)S(1)}, f32[2,16,128,1024]{2,3,1,0:T(8,128)}) fusion(pred[128,1024]{0,1:T(8,128)(4,1)S(1)} %iota_compare_fusion.1, bf16[1024,2,128,1]{0,2,3,1:T(8,128)(2,1)S(1)} %bitcast.104, bf16[128,2,16,128]{3,2,1,0:T(8,128)(2,1)S(1)} %bitcast.101), kind=kOutput, calls=%fused_computation.62 | convolution fusion | flops 1090520064 | bytes 18497536 | tf_op jit(solution)/shard_map/sub | solution.py:23
  45.9 7.1 %fusion.23 = bf16[2,16,128,128]{2,3,1,0:T(8,128)(2,1)S(1)} fusion(bf16[1024,2,128,1]{0,2,3,1:T(8,128)(2,1)S(1)} %bitcast.105, f32[2,16,128,1024]{2,3,1,0:T(8,128)} %get-tuple-element.8, f32[2,16,128]{2,1,0:T(8,128)S(1)} %get-tuple-element.7), kind=kOutput, calls=%fused_computation.32 | convolution fusion | flops 1082654720 | bytes 18366464 | tf_op jit(solution)/shard_map/kgrc,ckd->rkgd/dot_general | solution.py:25
  53.5 18.4 %all_to_all.29 = bf16[128,8,512]{2,0,1:T(8,128)(2,1)S(1)} all-to-all(bf16[128,8,512]{2,0,1:T(8,128)(2,1)S(1)} %copy.52), channel_id=1, replica_groups=mesh['group'=16,'tensor'=8] {'tensor'}, dimensions={1} | all-to-all | bytes 2097152 | tf_op jit(solution)/shard_map/all_to_all | solution.py:56
  71.9 10.3 %fusion.48 = f32[1024,4096]{1,0:T(8,128)} fusion(bf16[1024,512]{1,0:T(8,128)(2,1)S(1)} %bitcast.103, bf16[512,4096]{1,0:T(8,128)(2,1)} %param.14), kind=kOutput, calls=%fused_computation.63 | convolution fusion | flops 4294967296 | bytes 22020096 | tf_op jit(solution)/shard_map/dot_general | solution.py:58
  85.1 89.2 %reduce-scatter.2.cloned.1.call-done = f32[128,4096]{1,0:T(8,128)} async-done(((f32[1024,4096]{1,0:T(8,128)}), f32[128,4096]{1,0:T(8,128)}) %reduce-scatter.2.cloned.1.call-update) | async-done | bytes 2097168 | tf_op jit(solution)/shard_map/reduce_scatter | solution.py:57
  174.3 2.1 multiply_reduce_fusion.1
  176.5 3.3 fusion.15
  179.8 6.6 %broadcast_in_dim.39 = bf16[64,2,8,4096]{3,2,1,0:T(8,128)(2,1)} broadcast(bf16[64,8,4096]{2,1,0:T(8,128)(2,1)} %fusion.15), dimensions={0,2,3} | broadcast | bytes 12582912 | tf_op jit(solution)/shard_map/broadcast_in_dim | solution.py:82
  186.4 106.9 %all_to_all.30 = bf16[128,8,4096]{2,1,0:T(8,128)(2,1)S(1)} all-to-all(bf16[128,8,4096]{2,1,0:T(8,128)(2,1)} %bitcast.99), channel_id=1, replica_groups=mesh['group'=16,'tensor'=8] {'group','tensor'}, dimensions={0} | all-to-all | bytes 16777216 | tf_op jit(solution)/shard_map/all_to_all | solution.py:85
  293.4 8.3 %fusion.4 = f32[1024,768]{1,0:T(8,128)} fusion(bf16[128,8,4096]{2,1,0:T(8,128)(2,1)S(1)} %all_to_all.30, bf16[1,4096,768]{2,1,0:T(8,128)(2,1)S(1)} %bitcast.108), kind=kOutput, calls=%fused_computation.10 | convolution fusion | flops 6442450944 | bytes 17825792 | tf_op jit(solution)/shard_map/dot_general | solution.py:91
  301.7 8.8 %multiply_convert_fusion = bf16[1024,768]{1,0:T(8,128)(2,1)S(1)} fusion(f32[1024,768]{1,0:T(8,128)} %fusion.4, bf16[1,4096,768]{2,1,0:T(8,128)(2,1)S(1)} %bitcast.110, bf16[128,8,4096]{2,1,0:T(8,128)(2,1)S(1)} %all_to_all.30), kind=kOutput, calls=%fused_computation.26 | convolution fusion | flops 6447169536 | bytes 19398656 | tf_op jit(solution)/shard_map/dot_general | solution.py:90
  310.6 8.8 %convert_bitcast_fusion = bf16[128,8,4096]{2,1,0:T(8,128)(2,1)} fusion(bf16[1024,768]{1,0:T(8,128)(2,1)S(1)} %multiply_convert_fusion, bf16[1,768,4096]{2,1,0:T(8,128)(2,1)S(1)} %bitcast.112), kind=kOutput, calls=%fused_computation.15 | convolution fusion | flops 6446645248 | bytes 16252928 | tf_op jit(solution)/shard_map/dot_general | solution.py:93
  319.4 9.4 %all-to-all-start.2 = ((bf16[128,8,4096]{2,1,0:T(8,128)(2,1)}), bf16[128,8,4096]{2,1,0:T(8,128)(2,1)}, u32[]{:S(2)}, u32[]{:S(2)}) async-start(bf16[128,8,4096]{2,1,0:T(8,128)(2,1)} %convert_bitcast_fusion), calls=%async_computation.3 | async-start | bytes 16777216 | tf_op jit(solution)/shard_map/all_to_all | solution.py:95
  329.4 105.8 %all-to-all-done.2 = bf16[128,8,4096]{2,1,0:T(8,128)(2,1)} async-done(((bf16[128,8,4096]{2,1,0:T(8,128)(2,1)}), bf16[128,8,4096]{2,1,0:T(8,128)(2,1)}, u32[]{:S(2)}, u32[]{:S(2)}) %all-to-all-start.2) | async-done | bytes 8388640 | tf_op jit(solution)/shard_map/all_to_all | solution.py:95
  435.2 11.4 %convert.1 = f32[64,2,8,4096]{3,2,1,0:T(8,128)} convert(bf16[64,2,8,4096]{3,2,1,0:T(8,128)(2,1)} %bitcast.19) | non-fusion elementwise | flops 4194304 | bytes 25165824 | tf_op jit(solution)/shard_map/convert_element_type | solution.py:99
  446.6 8.4 %fusion.16 = bf16[64,8,4096]{2,1,0:T(8,128)(2,1)} fusion(f32[64,2,8,4096]{3,2,1,0:T(8,128)} %convert.1), kind=kLoop, calls=%fused_computation.25 | loop fusion | flops 4194304 | bytes 20971520 | tf_op jit(solution)/shard_map/convert_element_type | solution.py:101
  455.0 11.0 %gather_fusion = bf16[384,4096]{1,0:T(8,128)(2,1)} fusion(bf16[512,4096]{1,0:T(8,128)(2,1)} %bitcast.98, s32[1024]{0:T(1024)S(1)} %pad_clamp_fusion), kind=kCustom, calls=%fused_computation | custom fusion | bytes 6292992 | tf_op jit(solution)/shard_map/jit(_take)/gather | solution.py:104
  466.0 7.3 %gather.7 = bf16[128,3,4096]{2,1,0:T(4,128)(2,1)} reshape(bf16[384,4096]{1,0:T(8,128)(2,1)} %gather_fusion) | data formatting | bytes 6291456 | tf_op jit(solution)/shard_map/jit(_take)/gather | solution.py:104
  473.3 11.4 %multiply_reduce_fusion = f32[128,4096]{1,0:T(8,128)S(1)} fusion(f32[128,3]{1,0:T(8,128)S(1)} %copy.61, bf16[128,3,4096]{2,1,0:T(4,128)(2,1)} %gather.7, pred[128,3]{1,0:T(8,128)(4,1)S(1)} %copy.57), kind=kLoop, calls=%fused_computation.14 | loop fusion | flops 5767168 | bytes 5244800 | tf_op jit(solution)/shard_map/reduce_sum | solution.py:105
  484.7 1.4 add_convert_fusion
  (51 shorter events, 4.5 us)
Async XLA Ops:
  6.5 167.7 %reduce-scatter.2.cloned.1.call-start = ((), (), s32[]{:S(2)}) async-start(), calls=%async_computation.4 | async-start | bytes 18874368 | tf_op jit(solution)/shard_map/reduce_scatter | solution.py:57
  82.2 0.7 copy-start.2
  82.2 92.1 %copy-start.1 = (bf16[128,4096]{1,0:T(8,128)(2,1)S(1)}, bf16[128,4096]{1,0:T(8,128)(2,1)}, u32[]{:S(2)}) copy-start(bf16[128,4096]{1,0:T(8,128)(2,1)} %param.15) | copy-start | bytes 3145732
  82.9 93.5 %copy-start.3 = (f32[4096]{0:T(1024)S(1)}, f32[4096]{0:T(1024)}, u32[]{:S(2)}) copy-start(f32[4096]{0:T(1024)} %param.16) | copy-start | bytes 49156
  174.3 2.2 copy-start
  179.8 113.6 %slice-start = ((s8[6291456]{0:T(1024)(128)(4,1)}), s8[2097152]{0:T(1024)(128)(4,1)S(1)}, s32[]{:S(2)}) async-start(s8[6291456]{0:T(1024)(128)(4,1)} %bitcast.107), calls=%async_computation.5 | async-start | bytes 4194304
  186.4 106.9 %slice-start.1 = ((s8[6291456]{0:T(1024)(128)(4,1)}), s8[4194304]{0:T(1024)(128)(4,1)S(1)}, s32[]{:S(2)}) async-start(s8[6291456]{0:T(1024)(128)(4,1)} %bitcast.107), calls=%async_computation.6 | async-start | bytes 8388608
  186.4 115.3 %slice-start.2 = ((s8[6291456]{0:T(1024)(128)(4,1)}), s8[4194304]{0:T(1024)(128)(4,1)S(1)}, s32[]{:S(2)}) async-start(s8[6291456]{0:T(1024)(128)(4,1)} %bitcast.109), calls=%async_computation.7 | async-start | bytes 8388608
  293.4 8.4 %slice-start.3 = ((s8[6291456]{0:T(1024)(128)(4,1)}), s8[2097152]{0:T(1024)(128)(4,1)S(1)}, s32[]{:S(2)}) async-start(s8[6291456]{0:T(1024)(128)(4,1)} %bitcast.109), calls=%async_computation.8 | async-start | bytes 4194304
  293.4 17.2 %slice-start.4 = ((s8[6291456]{0:T(1024)(128)(4,1)}), s8[4194304]{0:T(1024)(128)(4,1)S(1)}, s32[]{:S(2)}) async-start(s8[6291456]{0:T(1024)(128)(4,1)} %bitcast.111), calls=%async_computation.9 | async-start | bytes 8388608
  301.7 8.8 %slice-start.5 = ((s8[6291456]{0:T(1024)(128)(4,1)}), s8[2097152]{0:T(1024)(128)(4,1)S(1)}, s32[]{:S(2)}) async-start(s8[6291456]{0:T(1024)(128)(4,1)} %bitcast.111), calls=%async_computation.10 | async-start | bytes 4194304
  319.4 9.9 %copy-start.4 = (f32[128,3]{0,1:T(4,128)S(1)}, f32[128,3]{0,1:T(4,128)}, u32[]{:S(2)}) copy-start(f32[128,3]{0,1:T(4,128)} %param.18) | copy-start | bytes 4612
  319.4 115.8 %all-to-all-start.2 = ((bf16[128,8,4096]{2,1,0:T(8,128)(2,1)}), bf16[128,8,4096]{2,1,0:T(8,128)(2,1)}, u32[]{:S(2)}, u32[]{:S(2)}) async-start(bf16[128,8,4096]{2,1,0:T(8,128)(2,1)} %convert_bitcast_fusion), calls=%async_computation.3 | async-start | bytes 16777216 | tf_op jit(solution)/shard_map/all_to_all | solution.py:95
Sparse Core Ops, SparseCore 0:
  82.3 91.8 reduce-scatter.1
where the time goes:
time: 502 us; the launch traced here: 493 us
  waiting for transfers between devices  195 us (39%)
  blocking collectives  153 us (30%)
  matrix products  55.6 us (11%)
  other arithmetic  35.9 us (7%)
  local copies, waits for them, and re-layouts  30.5 us (6%)
  between operations  14 us (3%)
  starting transfers between devices  9.41 us (2%)
    all_to_all x1, blocking collectives, local(): lax.all_to_all(doubled, ('group', 'tensor'), split_axis=0, concat_axis=0,...  107 us
    all_to_all x1, waiting for transfers between devices, local(): lax.all_to_all(pieces, ('group', 'tensor'), split_axis=0, concat_axis=0,...  106 us
    reduce_scatter x1, waiting for transfers between devices, local(): lax.psum_scatter(jnp.dot(context, out_weight, preferred_element_type=jnp....  89.2 us
    all_to_all x1, blocking collectives, local(): lax.all_to_all(own_context, 'tensor', split_axis=1, concat_axis=0, tiled=...  18.4 us
    gather x2, local copies, waits for them, and re-layouts, local(): jnp.take(flat_out, slot_index, axis=0).reshape(rows_here, TOP, width)  18.3 us
    all_gather x1, blocking collectives, local(): lax.all_gather(rotated_key_rows, 'tensor', axis=0, tiled=True)  14.3 us
    all_gather x1, blocking collectives, local(): lax.all_gather(value_row_matrix, 'tensor', axis=0, tiled=True)  13.3 us
    convert_element_type x1, other arithmetic, local(): returned = lax.optimization_barrier(returned).reshape(expert_count, 2, ca...  11.4 us
  transfers between devices with their start and end apart: 2, of which 2 were waited for; matrix products, arithmetic and copies ran while one was open for 1% of the time, Pallas kernels for 0%

commit v1 on v0

v1 whole, which is shorter than its diff:
```python
import jax
import jax.numpy as jnp
from jax import lax
from jax.experimental import pallas as pl
from jax.experimental.pallas import tpu as pltpu
from jax.sharding import PartitionSpec as P

HEAD = 128
TOP = 3
CAP = 8
AXES = ("group", "tensor")
LOG2E = 1.4426950408889634
ORDER = (2, 1, 3, 0)


def attention_kernel(where_ref, q_ref, k_ref, v_ref, o_ref):
    rows = q_ref.shape[1]
    heads = q_ref.shape[2] // HEAD
    place = where_ref[pl.program_id(0)]
    core = where_ref[4]
    scale = HEAD ** (-0.5) * LOG2E
    for block in range(4):

        @pl.when(place == block)
        def _():
            columns = 256 * (block + 1)
            keys = k_ref[0:columns, :]
            values = v_ref[0:columns, :]
            row = lax.broadcasted_iota(jnp.int32, (2 * rows, 256), 0) % rows
            column = lax.broadcasted_iota(jnp.int32, (2 * rows, 256), 1)
            allowed = column <= row + core * rows

            def pair(index, carry):
                start = pl.multiple_of(index * 2 * HEAD, 2 * HEAD)
                both = q_ref[0, :, pl.ds(start, 2 * HEAD)]
                q = jnp.concatenate([both[:, :HEAD], both[:, HEAD:]], axis=0)
                scores = lax.dot_general(
                    q, keys, (((1,), (1,)), ((), ())), preferred_element_type=jnp.float32
                )
                last = jnp.where(allowed, scores[:, columns - 256 :], -1e30)
                if block:
                    scores = jnp.concatenate([scores[:, : columns - 256], last], axis=1)
                else:
                    scores = last
                largest = jnp.max(scores, axis=1, keepdims=True)
                weights = jnp.exp2((scores - largest) * scale)
                total = jnp.sum(weights, axis=1, keepdims=True)
                context = jnp.dot(
                    weights.astype(jnp.bfloat16), values, preferred_element_type=jnp.float32
                )
                context = (context / total).astype(jnp.bfloat16)
                o_ref[0, :, pl.ds(start, 2 * HEAD)] = jnp.concatenate(
                    [context[:rows], context[rows:]], axis=1
                )
                return carry

            lax.fori_loop(0, heads // 2, pair, 0)


def attention(where, queries, keys, values):
    ring, rows, width = queries.shape
    return pl.pallas_call(
        attention_kernel,
        out_shape=jax.ShapeDtypeStruct((ring, rows, width), jnp.bfloat16),
        grid_spec=pltpu.PrefetchScalarGridSpec(
            num_scalar_prefetch=1,
            grid=(ring,),
            in_specs=[
                pl.BlockSpec((1, rows, width), lambda i, w: (i, 0, 0)),
                pl.BlockSpec(keys.shape, lambda i, w: (0, 0)),
                pl.BlockSpec(values.shape, lambda i, w: (0, 0)),
            ],
            out_specs=pl.BlockSpec((1, rows, width), lambda i, w: (i, 0, 0)),
        ),
        compiler_params=pltpu.CompilerParams(vmem_limit_bytes=32 * 1024 * 1024),
        cost_estimate=pl.CostEstimate(
            flops=2 * 2 * 8 * rows * 2560 * HEAD, bytes_accessed=3 << 20, transcendentals=8 * rows * 2560
        ),
    )(where, queries, keys, values)


def fdot(a, b):
    return jnp.dot(a, b, preferred_element_type=jnp.float32)


def local(
    queries,
    rotated_key_rows,
    value_row_matrix,
    out_weight,
    residual,
    norm_gain,
    expert_ids,
    gate_weights,
    w_gate,
    w_up,
    w_down,
):
    bf16, f32 = jnp.bfloat16, jnp.float32
    rows = queries.shape[0]
    width = residual.shape[1]
    tensor = lax.axis_size("tensor")
    devices = lax.axis_size("group") * tensor
    experts = devices // 2
    place = lax.axis_index("tensor")
    y, core = place // 2, place % 2
    other = 1 - core
    ring = tensor // 2
    chip_width = queries.shape[1] // ring
    half_width = chip_width // 2
    half = width // 2

    def along(value, step):
        return lax.ppermute(value, "tensor", [(i, (i + 2 * step) % tensor) for i in range(tensor)])

    def swap(value):
        return lax.ppermute(value, "tensor", [(i, i ^ 1) for i in range(tensor)])

    def columns(value, start, size):
        return lax.dynamic_slice_in_dim(value, start, size, axis=1)

    weight_other = swap(out_weight)

    def outgoing(step):
        to = (y + step) % ring
        key_head = to * rotated_key_rows.shape[1] // HEAD // ring * HEAD
        return jnp.concatenate(
            [
                columns(queries, to * chip_width + core * half_width, half_width),
                columns(queries, to * chip_width + other * half_width, half_width),
                columns(rotated_key_rows, key_head, HEAD),
                columns(value_row_matrix, key_head, HEAD),
            ],
            axis=1,
        )

    arrived = [outgoing(0)] + [along(outgoing(step), step) for step in (1, 2, 3)]
    stacked = jnp.stack([arrived[(-s) % ring] for s in ORDER])
    key_values = stacked[:, :, chip_width:]
    key_values_other = swap(key_values)
    places = (y + jnp.array(ORDER, jnp.int32)) % ring
    gathered = jnp.where(
        core == 0,
        jnp.stack([key_values, key_values_other], axis=1),
        jnp.stack([key_values_other, key_values], axis=1),
    )
    slot_of = jnp.array([ORDER.index(s) for s in range(ring)], jnp.int32)
    gathered = jnp.take(gathered, jnp.take(slot_of, (jnp.arange(ring) - y) % ring), axis=0)
    gathered = gathered.reshape(ring * 2 * rows, 2 * HEAD)
    where = jnp.concatenate([places, core[None]]).astype(jnp.int32)
    context = attention(where, stacked[:, :, :chip_width], gathered[:, :HEAD], gathered[:, HEAD:])

    def project(block):
        return fdot(block[:, :half_width], out_weight) + fdot(block[:, half_width:], weight_other)

    opposite = project(context[0]).astype(bf16)
    from_left = along(opposite[:, :half], 1)
    from_right = along(opposite[:, half:], -1)
    right = project(context[1])
    left = project(context[2])
    right_plain = along(right[:, half:].astype(bf16), 1)
    left_plain = along(left[:, :half].astype(bf16), -1)
    right_sum = along((right[:, :half] + from_left.astype(f32)).astype(bf16), 1)
    left_sum = along((left[:, half:] + from_right.astype(f32)).astype(bf16), -1)
    own = project(context[3])
    hidden = residual.astype(f32) + own
    hidden = hidden + jnp.concatenate(
        [
            right_sum.astype(f32) + left_plain.astype(f32),
            right_plain.astype(f32) + left_sum.astype(f32),
        ],
        axis=1,
    )

    mean_square = jnp.mean(hidden * hidden, axis=-1, keepdims=True)
    moe_input = (hidden * lax.rsqrt(mean_square + 1e-06) * norm_gain).astype(bf16)

    flat_ids = expert_ids.reshape(-1)
    one_hot = (flat_ids[:, None] == jnp.arange(experts, dtype=jnp.int32)[None, :]).astype(jnp.int32)
    earlier = jnp.cumsum(one_hot, axis=0) - one_hot
    rank_within = jnp.sum(earlier * one_hot, axis=1)
    slot_index = (flat_ids * (2 * CAP) + rank_within).reshape(rows, TOP)
    slot_rows = jnp.arange(2 * experts * CAP, dtype=jnp.int32)[:, None]
    hit = [
        [slot_rows == slot_index[:, k][None, :] + side * CAP for k in range(TOP)] for side in (0, 1)
    ]
    selector = jnp.concatenate([h[0] | h[1] | h[2] for h in hit], axis=1).astype(bf16)
    spread = jnp.concatenate(
        [
            sum(jnp.where(h[k], gate_weights[:, k][None, :], 0.0) for k in range(TOP))
            for h in hit
        ],
        axis=1,
    )
    spread_high = spread.astype(bf16)
    spread_low = (spread - spread_high.astype(f32)).astype(bf16)

    halves = jnp.concatenate([moe_input[:, :half], moe_input[:, half:]], axis=0)
    slots = fdot(selector, halves).astype(bf16).reshape(devices, CAP, half)
    mine = lax.all_to_all(slots, AXES, split_axis=0, concat_axis=0, tiled=True)
    mine = mine.reshape(devices * CAP, half)
    theirs = swap(mine)

    def rows_of(weight, side):
        return lax.dynamic_slice_in_dim(weight[0], side * half, half, axis=0)

    gate = fdot(mine, rows_of(w_gate, core))
    upward = fdot(mine, rows_of(w_up, core))
    gate = gate + fdot(theirs, rows_of(w_gate, other))
    upward = upward + fdot(theirs, rows_of(w_up, other))
    activation = (jax.nn.silu(gate) * upward).astype(bf16)
    to_other = fdot(activation, columns(w_down[0], other * half, half)).astype(bf16)
    part_other = swap(to_other)
    part_own = fdot(activation, columns(w_down[0], core * half, half)).astype(bf16)
    expert_out = (part_own.astype(f32) + part_other.astype(f32)).astype(bf16)
    returned = lax.all_to_all(
        expert_out.reshape(devices, CAP, half), AXES, split_axis=0, concat_axis=0, tiled=True
    ).reshape(devices * CAP, half)

    def gather_back(weights):
        return lax.dot_general(
            weights, returned, (((0,), (0,)), ((), ())), preferred_element_type=f32
        )

    routed = gather_back(spread_high) + gather_back(spread_low)
    routed = jnp.concatenate([routed[:rows], routed[rows:]], axis=1)
    return (hidden + routed).astype(bf16)


def solution(mesh):
    wide = P(AXES, None)
    return jax.shard_map(
        local,
        mesh=mesh,
        in_specs=(
            wide,
            wide,
            wide,
            P("tensor", None),
            wide,
            P(),
            wide,
            wide,
            P(AXES, None, None),
            P(AXES, None, None),
            P(AXES, None, None),
        ),
        out_specs=wide,
        check_vma=False,
    )
```

time: 502 us -> 266 us (0.53); the launches traced: 493 us -> 266 us
  waiting for transfers between devices: 195 us -> 94.7 us
  blocking collectives: 153 us -> 62.6 us
  other arithmetic: 35.9 us -> 4.44 us
  local copies, waits for them, and re-layouts: 30.5 us -> 5.43 us
  starting transfers between devices: 9.41 us -> 22.8 us
  between operations: 14 us -> 0.8 us
  Pallas kernels: 0 us -> 9.64 us
  matrix products: 55.6 us -> 65.1 us
    reduce_scatter x1 -> x0, waiting for transfers between devices: 89.2 us -> none  [local(): lax.psum_scatter(jnp.dot(context, out_weight, preferred_element_type=jnp....]
    all_to_all x2 -> x1, blocking collectives: 125 us -> 62.6 us  [local(): mine = lax.all_to_all(slots, AXES, split_axis=0, concat_axis=0, tiled=True)]
    all_to_all x1, waiting for transfers between devices: 106 us -> 52 us  [local(): lax.all_to_all(expert_out.reshape(devices, CAP, half), AXES, split_axis=0...]
    ppermute x0 -> x13, waiting for transfers between devices: none -> 42.7 us  [the longest x9 34.7 us: along(): lax.ppermute(value, 'tensor', [(i, (i + 2 * step) % tensor) for i in rang...]
    all_gather x2 -> x0, blocking collectives: 27.6 us -> none  [the longest x1 14.3 us: local(): lax.all_gather(rotated_key_rows, 'tensor', axis=0, tiled=True)]
    convert_element_type x4 -> x5, other arithmetic: 21.2 us -> 1.77 us  [the longest x1 1.24 us: local(): return (hidden + routed).astype(bf16)]
    dot_general x6 -> x17, matrix products: 46.6 us -> 65.1 us  [the longest x15 58.1 us: fdot(): return jnp.dot(a, b, preferred_element_type=jnp.float32)]
    ppermute x0 -> x13, starting transfers between devices: none -> 17.6 us  [the longest x9 13.2 us: along(): lax.ppermute(value, 'tensor', [(i, (i + 2 * step) % tensor) for i in rang...]
  transfers between devices with their start and end apart: 2 -> 14, of which waited for: 2 -> 9; matrix products, arithmetic and copies ran while one was open for 1% -> 13% of each run, Pallas kernels for 0% -> 4%
where the time goes in v1:
time: 266 us
  waiting for transfers between devices  94.7 us (36%)
  matrix products  65.1 us (24%)
  blocking collectives  62.6 us (24%)
  starting transfers between devices  22.8 us (9%)
  Pallas kernels  9.64 us (4%)
  local copies, waits for them, and re-layouts  5.43 us (2%)
  other arithmetic  4.44 us (2%)
    all_to_all x1, blocking collectives, local(): mine = lax.all_to_all(slots, AXES, split_axis=0, concat_axis=0, tiled=True)  62.6 us
    dot_general x15, matrix products, fdot(): return jnp.dot(a, b, preferred_element_type=jnp.float32)  58.1 us
    all_to_all x1, waiting for transfers between devices, local(): lax.all_to_all(expert_out.reshape(devices, CAP, half), AXES, split_axis=0...  52 us
    ppermute x9, waiting for transfers between devices, along(): lax.ppermute(value, 'tensor', [(i, (i + 2 * step) % tensor) for i in rang...  34.7 us
    ppermute x9, starting transfers between devices, along(): lax.ppermute(value, 'tensor', [(i, (i + 2 * step) % tensor) for i in rang...  13.2 us
    pallas_call x1, Pallas kernels, attention(): pl.pallas_call(attention_kernel, out_shape=jax.ShapeDtypeStruct((ring, ro...  9.64 us
    ppermute x4, waiting for transfers between devices, swap(): return lax.ppermute(value, 'tensor', [(i, i ^ 1) for i in range(tensor)])  7.98 us
    dot_general x2, matrix products, gather_back(): lax.dot_general(weights, returned, (((0,), (0,)), ((), ())), preferred_el...  6.96 us
  transfers between devices with their start and end apart: 14, of which 9 were waited for; matrix products, arithmetic and copies ran while one was open for 13% of the time, Pallas kernels for 4%

profile of v1, /device:TPU:1, one launch (start us, length us, event | category | flops | bytes accessed | tf_op | source)
XLA Modules:
  0.0 265.5 jit_solution(7003534756433600849)
XLA Ops:
  13.6 7.9 %collective-permute-done = bf16[128,1280]{1,0:T(8,128)(2,1)S(1)} collective-permute-done((bf16[128,1280]{1,0:T(8,128)(2,1)S(1)}, bf16[128,1280]{1,0:T(8,128)(2,1)S(1)}, u32[]{:S(2)}, u32[]{:S(2)}) %collective-permute-start) | collective-permute-done | bytes 327712 | tf_op jit(solution)/shard_map/ppermute | solution.py:114
  25.3 9.6 %shard_map.127 = bf16[4,128,1024]{2,1,0:T(8,128)(2,1)S(1)} custom-call(s32[5]{0:T(128)S(1)} %pad_add_fusion.where_ref, bf16[4,128,1024]{2,1,0:T(8,128)(2,1)S(1)} %slice.148.q_ref, bf16[1024,128]{1,0:T(8,128)(2,1)S(1)} %get-tuple-element.24.k_ref, bf16[1024,128]{1,0:T(8,128)(2,1)S(1)} %get-tuple-element.23.v_ref), custom_call_target="tpu_custom_call" | custom-call | flops 1342177280 | bytes 3145728 | tf_op jit(solution)/shard_map/pallas_call | solution.py:62
  37.9 2.9 %fusion.48 = f32[128,4096]{1,0:T(8,128)S(1)} fusion(bf16[512,4096]{1,0:T(8,128)(2,1)} %param.16, bf16[128,1024]{1,0:T(8,128)(2,1)S(1)} %get-tuple-element.13), kind=kOutput, calls=%fused_computation.84 | convolution fusion | flops 536870912 | bytes 6422528 | tf_op jit(solution)/shard_map/dot_general | solution.py:83
  40.8 2.9 %fusion.51 = f32[128,4096]{1,0:T(8,128)S(1)} fusion(bf16[512,4096]{1,0:T(8,128)(2,1)} %param.16, bf16[128,1024]{1,0:T(8,128)(2,1)S(1)} %get-tuple-element.11), kind=kOutput, calls=%fused_computation.87 | convolution fusion | flops 536870912 | bytes 6422528 | tf_op jit(solution)/shard_map/dot_general | solution.py:83
  43.7 3.0 %fusion.2 = bf16[128,4096]{1,0:T(8,128)(2,1)S(1)} fusion(f32[128,4096]{1,0:T(8,128)S(1)} %fusion.48, bf16[512,4096]{1,0:T(8,128)(2,1)} %collective-permute-done.4, bf16[128,1024]{1,0:T(8,128)(2,1)S(1)} %get-tuple-element.13), kind=kOutput, calls=%fused_computation.9 | convolution fusion | flops 537919488 | bytes 7471104 | tf_op jit(solution)/shard_map/dot_general | solution.py:83
  48.5 3.0 %convolution_add_fusion.2 = f32[128,4096]{1,0:T(8,128)S(1)} fusion(f32[128,4096]{1,0:T(8,128)S(1)} %fusion.51, bf16[512,4096]{1,0:T(8,128)(2,1)} %collective-permute-done.4, bf16[128,1024]{1,0:T(8,128)(2,1)S(1)} %get-tuple-element.11), kind=kOutput, calls=%fused_computation.5 | convolution fusion | flops 537395200 | bytes 8519680 | tf_op jit(solution)/shard_map/dot_general | solution.py:83
  52.4 3.0 %convolution_add_fusion = f32[128,4096]{1,0:T(8,128)S(1)} fusion(f32[128,4096]{1,0:T(8,128)S(1)} %fusion.45, bf16[512,4096]{1,0:T(8,128)(2,1)} %collective-permute-done.4, bf16[128,1024]{1,0:T(8,128)(2,1)S(1)} %get-tuple-element.12), kind=kOutput, calls=%fused_computation.3 | convolution fusion | flops 537395200 | bytes 8519680 | tf_op jit(solution)/shard_map/dot_general | solution.py:83
  60.2 3.1 %collective-permute-start.10 = (bf16[128,2048]{1,0:T(8,128)(2,1)S(1)}, bf16[128,2048]{1,0:T(8,128)(2,1)S(1)}, u32[]{:S(2)}, u32[]{:S(2)}) collective-permute-start(bf16[128,2048]{1,0:T(8,128)(2,1)S(1)} %fusion.30), channel_id=1, source_target_pairs={{0,6},{1,7},{2,0},{3,1},{4,2},{5,3},{6,4},{7,5},{8,14},{9,15},{10,... | collective-permute-start | bytes 1572872 | tf_op jit(solution)/shard_map/ppermute | solution.py:114
  63.2 13.7 %collective-permute-done.5 = bf16[128,2048]{1,0:T(8,128)(2,1)S(1)} collective-permute-done((bf16[128,2048]{1,0:T(8,128)(2,1)S(1)}, bf16[128,2048]{1,0:T(8,128)(2,1)S(1)}, u32[]{:S(2)}, u32[]{:S(2)}) %collective-permute-start.5) | collective-permute-done | bytes 524320 | tf_op jit(solution)/shard_map/ppermute | solution.py:114
  77.1 2.9 %fusion.54 = f32[128,4096]{1,0:T(8,128)S(1)} fusion(bf16[512,4096]{1,0:T(8,128)(2,1)} %param.16, bf16[128,1024]{1,0:T(8,128)(2,1)S(1)} %get-tuple-element.14), kind=kOutput, calls=%fused_computation.90 | convolution fusion | flops 536870912 | bytes 6422528 | tf_op jit(solution)/shard_map/dot_general | solution.py:83
  82.7 7.6 %collective-permute-done.6 = bf16[128,2048]{1,0:T(8,128)(2,1)S(1)} collective-permute-done((bf16[128,2048]{1,0:T(8,128)(2,1)S(1)}, bf16[128,2048]{1,0:T(8,128)(2,1)S(1)}, u32[]{:S(2)}, u32[]{:S(2)}) %collective-permute-start.6) | collective-permute-done | bytes 524320 | tf_op jit(solution)/shard_map/ppermute | solution.py:114
  90.4 3.5 %multiply_reduce_fusion = (f32[128]{0:T(128)S(1)}, f32[128,4096]{1,0:T(8,128)S(1)}) fusion(f32[128,2048]{1,0:T(8,128)S(1)} %convert_add_fusion, f32[128,2048]{1,0:T(8,128)S(1)} %convert_add_fusion.1, f32[128,4096]{1,0:T(8,128)S(1)} %fusion.54, bf16[512,4096]{1,0:T(8,128)(2,1)} %collective-permute-done.4, bf16[128,1024]{1,0:T(8,128)(2,1)S(1)} %get-tuple-element.14, ...), kind=kOutput, calls=%fused_computation.38 | convolution fusion | flops 540540800 | bytes 11665920 | tf_op jit(solution)/shard_map/dot_general | solution.py:83
  95.6 62.6 %all_to_all.10 = bf16[128,8,2048]{2,1,0:T(8,128)(2,1)} all-to-all(bf16[128,8,2048]{2,1,0:T(8,128)(2,1)S(1)} %convert_bitcast_fusion), channel_id=1, replica_groups=mesh['group'=16,'tensor'=8] {'group','tensor'}, dimensions={0} | all-to-all | bytes 8388608 | tf_op jit(solution)/shard_map/all_to_all | solution.py:200
  159.5 6.3 %fusion.12 = f32[1024,768]{1,0:T(8,128)S(1)} fusion(bf16[1,4096,768]{2,1,0:T(8,128)(2,1)} %param.22, s32[]{:T(128)S(6)} %select_n.256, bf16[128,8,2048]{2,1,0:T(8,128)(2,1)} %all_to_all.10), kind=kOutput, calls=%fused_computation.21 | convolution fusion | flops 3221225472 | bytes 10485764 | tf_op jit(solution)/shard_map/dot_general | solution.py:83
  165.8 6.3 %fusion.16 = f32[1024,768]{1,0:T(8,128)S(1)} fusion(bf16[1,4096,768]{2,1,0:T(8,128)(2,1)} %param.21, s32[]{:T(128)S(6)} %select_n.256, bf16[128,8,2048]{2,1,0:T(8,128)(2,1)} %all_to_all.10), kind=kOutput, calls=%fused_computation.25 | convolution fusion | flops 3221225472 | bytes 10485764 | tf_op jit(solution)/shard_map/dot_general | solution.py:83
  172.2 5.4 %fusion.14 = f32[1024,768]{1,0:T(8,128)S(1)} fusion(bf16[1024,2048]{1,0:T(8,128)(2,1)} %collective-permute-done.11, bf16[1,4096,768]{2,1,0:T(8,128)(2,1)S(1)} %bitcast.125, s32[]{:T(128)S(6)} %select_n.257), kind=kOutput, calls=%fused_computation.23 | convolution fusion | flops 3221225472 | bytes 10485764 | tf_op jit(solution)/shard_map/dot_general | solution.py:83
  177.6 6.1 %multiply_convert_fusion = bf16[1024,768]{1,0:T(8,128)(2,1)S(1)} fusion(f32[1024,768]{1,0:T(8,128)S(1)} %fusion.12, f32[1024,768]{1,0:T(8,128)S(1)} %fusion.16, f32[1024,768]{1,0:T(8,128)S(1)} %fusion.14, bf16[1024,2048]{1,0:T(8,128)(2,1)} %collective-permute-done.11, bf16[1,4096,768]{2,1,0:T(8,128)(2,1)S(1)} %bitcast.127, s32[]{:T(128)S(6)} %select_n.257), kind=kOutput, calls=%fused_computation.29 | convolution fusion | flops 3227516928 | bytes 18350084 | tf_op jit(solution)/shard_map/dot_general | solution.py:83
  183.8 3.6 %convolution_convert_fusion = bf16[1024,2048]{1,0:T(8,128)(2,1)S(1)} fusion(bf16[1024,768]{1,0:T(8,128)(2,1)S(1)} %multiply_convert_fusion, bf16[1,768,4096]{2,1,0:T(8,128)(2,1)S(1)} %bitcast.129, s32[]{:T(128)S(6)} %select_n.257), kind=kOutput, calls=%fused_computation.16 | convolution fusion | flops 3223322624 | bytes 8912900 | tf_op jit(solution)/shard_map/dot_general | solution.py:83
  187.5 7.1 %collective-permute-done.12 = bf16[1024,2048]{1,0:T(8,128)(2,1)S(1)} collective-permute-done((bf16[1024,2048]{1,0:T(8,128)(2,1)S(1)}, bf16[1024,2048]{1,0:T(8,128)(2,1)S(1)}, u32[]{:S(2)}, u32[]{:S(2)}) %collective-permute-start.12) | collective-permute-done | bytes 4194336 | tf_op jit(solution)/shard_map/ppermute | solution.py:117
  194.7 5.0 %fusion.3 = bf16[128,8,2048]{2,1,0:T(8,128)(2,1)} fusion(bf16[1024,2048]{1,0:T(8,128)(2,1)S(1)} %collective-permute-done.12, bf16[1024,768]{1,0:T(8,128)(2,1)S(1)} %multiply_convert_fusion, bf16[1,768,4096]{2,1,0:T(8,128)(2,1)S(1)} %bitcast.129, s32[]{:T(128)S(6)} %select_n.256), kind=kOutput, calls=%fused_computation.10 | convolution fusion | flops 3231711232 | bytes 13107204 | tf_op jit(solution)/shard_map/dot_general | solution.py:83
  199.7 5.2 %all-to-all-start.1 = ((bf16[128,8,2048]{2,1,0:T(8,128)(2,1)}), bf16[128,8,2048]{2,1,0:T(8,128)(2,1)}, u32[]{:S(2)}, u32[]{:S(2)}) async-start(bf16[128,8,2048]{2,1,0:T(8,128)(2,1)} %fusion.3), calls=%async_computation.1 | async-start | bytes 8388608 | tf_op jit(solution)/shard_map/all_to_all | solution.py:216
  205.2 52.0 %all-to-all-done.1 = bf16[128,8,2048]{2,1,0:T(8,128)(2,1)} async-done(((bf16[128,8,2048]{2,1,0:T(8,128)(2,1)}), bf16[128,8,2048]{2,1,0:T(8,128)(2,1)}, u32[]{:S(2)}, u32[]{:S(2)}) %all-to-all-start.1) | async-done | bytes 4194336 | tf_op jit(solution)/shard_map/all_to_all | solution.py:216
  257.2 3.5 %fusion.4 = f32[256,2048]{1,0:T(8,128)S(1)} fusion(bf16[128,8,2048]{2,1,0:T(8,128)(2,1)} %all-to-all-done.1, f32[1024,128]{1,0:T(8,128)S(1)} %get-tuple-element.43, f32[1024,128]{1,0:T(8,128)S(1)} %get-tuple-element.42), kind=kOutput, calls=%fused_computation.11 | convolution fusion | flops 1075052544 | bytes 7340032 | tf_op jit(solution)/shard_map/dot_general | solution.py:221
  260.7 3.5 %fusion.24 = f32[256,2048]{1,0:T(8,128)S(1)} fusion(f32[256,2048]{1,0:T(8,128)S(1)} %fusion.4, bf16[128,8,2048]{2,1,0:T(8,128)(2,1)} %all-to-all-done.1, f32[1024,128]{1,0:T(8,128)S(1)} %get-tuple-element.43, f32[1024,128]{1,0:T(8,128)S(1)} %get-tuple-element.42), kind=kOutput, calls=%fused_computation.34 | convolution fusion | flops 1075314688 | bytes 9437184 | tf_op jit(solution)/shard_map/dot_general | solution.py:221
  (103 shorter events, 35.1 us)
Async XLA Ops:
  0.0 9.6 %copy-start = (s32[4]{0:T(128)S(1)}, s32[4]{0:T(128)}, u32[]{:S(2)}) copy-start(s32[4]{0:T(128)} %constant.195.clone) | copy-start | bytes 52
  0.0 10.3 %copy-start.3 = (s32[128,3]{0,1:T(4,128)S(1)}, s32[128,3]{0,1:T(4,128)}, u32[]{:S(2)}) copy-start(s32[128,3]{0,1:T(4,128)} %param.19) | copy-start | bytes 4612
  0.0 12.5 %copy-start.5 = (s32[4]{0:T(128)S(1)}, s32[4]{0:T(128)}, u32[]{:S(2)}) copy-start(s32[4]{0:T(128)} %constant.194.clone) | copy-start | bytes 52
  2.6 11.1 %collective-permute-start.2 = (bf16[128,1280]{1,0:T(8,128)(2,1)S(1)}, bf16[128,1280]{1,0:T(8,128)(2,1)S(1)}, u32[]{:S(2)}, u32[]{:S(2)}) collective-permute-start(bf16[128,1280]{1,0:T(8,128)(2,1)S(1)} %pad_maximum_fusion.4), channel_id=1, source_target_pairs={{0,2},{1,3},{2,4},{3,5},{4,6},{5,7},{6,0},{7,1},{8,10},{9,11},{10,... | collective-permute-start | bytes 983048 | tf_op jit(solution)/shard_map/ppermute | solution.py:114
  4.8 8.9 %collective-permute-start.1 = (bf16[128,1280]{1,0:T(8,128)(2,1)S(1)}, bf16[128,1280]{1,0:T(8,128)(2,1)S(1)}, u32[]{:S(2)}, u32[]{:S(2)}) collective-permute-start(bf16[128,1280]{1,0:T(8,128)(2,1)S(1)} %pad_maximum_fusion.3), channel_id=1, source_target_pairs={{0,6},{1,7},{2,0},{3,1},{4,2},{5,3},{6,4},{7,5},{8,14},{9,15},{10,... | collective-permute-start | bytes 983048 | tf_op jit(solution)/shard_map/ppermute | solution.py:114
  6.3 15.2 %collective-permute-start = (bf16[128,1280]{1,0:T(8,128)(2,1)S(1)}, bf16[128,1280]{1,0:T(8,128)(2,1)S(1)}, u32[]{:S(2)}, u32[]{:S(2)}) collective-permute-start(bf16[128,1280]{1,0:T(8,128)(2,1)S(1)} %pad_maximum_fusion.2), channel_id=1, source_target_pairs={{0,4},{1,5},{2,6},{3,7},{4,0},{5,1},{6,2},{7,3},{8,12},{9,13},{10,... | collective-permute-start | bytes 983048 | tf_op jit(solution)/shard_map/ppermute | solution.py:114
  8.1 35.7 %collective-permute-start.4 = (bf16[512,4096]{1,0:T(8,128)(2,1)}, bf16[512,4096]{1,0:T(8,128)(2,1)}, u32[]{:S(2)}, u32[]{:S(2)}) collective-permute-start(bf16[512,4096]{1,0:T(8,128)(2,1)} %param.16), channel_id=1, source_target_pairs={{0,1},{1,0},{2,3},{3,2},{4,5},{5,4},{6,7},{7,6},{8,9},{9,8},{10,11... | collective-permute-start | bytes 12582920 | tf_op jit(solution)/shard_map/ppermute | solution.py:117
  21.5 2.8 %collective-permute-start.3 = (bf16[4,128,256]{2,1,0:T(8,128)(2,1)S(1)}, bf16[4,128,256]{2,1,0:T(8,128)(2,1)S(1)}, u32[]{:S(2)}, u32[]{:S(2)}) collective-permute-start(bf16[4,128,256]{2,1,0:T(8,128)(2,1)S(1)} %pad_maximum_fusion.5), channel_id=1, source_target_pairs={{0,1},{1,0},{2,3},{3,2},{4,5},{5,4},{6,7},{7,6},{8,9},{9,8},{10,11... | collective-permute-start | bytes 786440 | tf_op jit(solution)/shard_map/ppermute | solution.py:117
  46.8 13.2 %collective-permute-start.9 = (bf16[128,2048]{1,0:T(8,128)(2,1)S(1)}, bf16[128,2048]{1,0:T(8,128)(2,1)S(1)}, u32[]{:S(2)}, u32[]{:S(2)}) collective-permute-start(bf16[128,2048]{1,0:T(8,128)(2,1)S(1)} %get-tuple-element.10), channel_id=1, source_target_pairs={{0,6},{1,7},{2,0},{3,1},{4,2},{5,3},{6,4},{7,5},{8,14},{9,15},{10,... | collective-permute-start | bytes 1572872 | tf_op jit(solution)/shard_map/ppermute | solution.py:114
  51.6 28.5 %collective-permute-start.8 = (bf16[128,2048]{1,0:T(8,128)(2,1)S(1)}, bf16[128,2048]{1,0:T(8,128)(2,1)S(1)}, u32[]{:S(2)}, u32[]{:S(2)}) collective-permute-start(bf16[128,2048]{1,0:T(8,128)(2,1)S(1)} %slice.215), channel_id=1, source_target_pairs={{0,2},{1,3},{2,4},{3,5},{4,6},{5,7},{6,0},{7,1},{8,10},{9,11},{10,... | collective-permute-start | bytes 1572872 | tf_op jit(solution)/shard_map/ppermute | solution.py:114
  51.7 25.3 %collective-permute-start.5 = (bf16[128,2048]{1,0:T(8,128)(2,1)S(1)}, bf16[128,2048]{1,0:T(8,128)(2,1)S(1)}, u32[]{:S(2)}, u32[]{:S(2)}) collective-permute-start(bf16[128,2048]{1,0:T(8,128)(2,1)S(1)} %get-tuple-element.9), channel_id=1, source_target_pairs={{0,2},{1,3},{2,4},{3,5},{4,6},{5,7},{6,0},{7,1},{8,10},{9,11},{10,... | collective-permute-start | bytes 1572872 | tf_op jit(solution)/shard_map/ppermute | solution.py:114
  55.5 27.2 %collective-permute-start.7 = (bf16[128,2048]{1,0:T(8,128)(2,1)S(1)}, bf16[128,2048]{1,0:T(8,128)(2,1)S(1)}, u32[]{:S(2)}, u32[]{:S(2)}) collective-permute-start(bf16[128,2048]{1,0:T(8,128)(2,1)S(1)} %slice.216), channel_id=1, source_target_pairs={{0,6},{1,7},{2,0},{3,1},{4,2},{5,3},{6,4},{7,5},{8,14},{9,15},{10,... | collective-permute-start | bytes 1572872 | tf_op jit(solution)/shard_map/ppermute | solution.py:114
  60.2 22.3 %collective-permute-start.10 = (bf16[128,2048]{1,0:T(8,128)(2,1)S(1)}, bf16[128,2048]{1,0:T(8,128)(2,1)S(1)}, u32[]{:S(2)}, u32[]{:S(2)}) collective-permute-start(bf16[128,2048]{1,0:T(8,128)(2,1)S(1)} %fusion.30), channel_id=1, source_target_pairs={{0,6},{1,7},{2,0},{3,1},{4,2},{5,3},{6,4},{7,5},{8,14},{9,15},{10,... | collective-permute-start | bytes 1572872 | tf_op jit(solution)/shard_map/ppermute | solution.py:114
  77.0 13.2 %collective-permute-start.6 = (bf16[128,2048]{1,0:T(8,128)(2,1)S(1)}, bf16[128,2048]{1,0:T(8,128)(2,1)S(1)}, u32[]{:S(2)}, u32[]{:S(2)}) collective-permute-start(bf16[128,2048]{1,0:T(8,128)(2,1)S(1)} %fusion.31), channel_id=1, source_target_pairs={{0,2},{1,3},{2,4},{3,5},{4,6},{5,7},{6,0},{7,1},{8,10},{9,11},{10,... | collective-permute-start | bytes 1572872 | tf_op jit(solution)/shard_map/ppermute | solution.py:114
  80.0 10.3 %copy-start.1 = (bf16[128,4096]{1,0:T(8,128)(2,1)S(1)}, bf16[128,4096]{1,0:T(8,128)(2,1)}, u32[]{:S(2)}) copy-start(bf16[128,4096]{1,0:T(8,128)(2,1)} %param.17) | copy-start | bytes 3145732
  158.2 13.9 %collective-permute-start.11 = (bf16[1024,2048]{1,0:T(8,128)(2,1)}, bf16[1024,2048]{1,0:T(8,128)(2,1)}, u32[]{:S(2)}, u32[]{:S(2)}) collective-permute-start(bf16[1024,2048]{1,0:T(8,128)(2,1)} %bitcast.23), channel_id=1, source_target_pairs={{0,1},{1,0},{2,3},{3,2},{4,5},{5,4},{6,7},{7,6},{8,9},{9,8},{10,11... | collective-permute-start | bytes 12582920 | tf_op jit(solution)/shard_map/ppermute | solution.py:117
  159.5 12.7 %slice-start = ((s8[6291456]{0:T(1024)(128)(4,1)}), s8[4194304]{0:T(1024)(128)(4,1)S(1)}, s32[]{:S(2)}) async-start(s8[6291456]{0:T(1024)(128)(4,1)} %bitcast.124), calls=%async_computation.2 | async-start | bytes 8388608
  159.5 18.1 %slice-start.2 = ((s8[6291456]{0:T(1024)(128)(4,1)}), s8[4194304]{0:T(1024)(128)(4,1)S(1)}, s32[]{:S(2)}) async-start(s8[6291456]{0:T(1024)(128)(4,1)} %bitcast.126), calls=%async_computation.4 | async-start | bytes 8388608
  165.8 6.4 %slice-start.1 = ((s8[6291456]{0:T(1024)(128)(4,1)}), s8[2097152]{0:T(1024)(128)(4,1)S(1)}, s32[]{:S(2)}) async-start(s8[6291456]{0:T(1024)(128)(4,1)} %bitcast.124), calls=%async_computation.3 | async-start | bytes 4194304
  165.8 11.8 %slice-start.3 = ((s8[6291456]{0:T(1024)(128)(4,1)}), s8[2097152]{0:T(1024)(128)(4,1)S(1)}, s32[]{:S(2)}) async-start(s8[6291456]{0:T(1024)(128)(4,1)} %bitcast.126), calls=%async_computation.5 | async-start | bytes 4194304
  165.8 18.0 %slice-start.4 = ((s8[6291456]{0:T(1024)(128)(4,1)}), s8[4194304]{0:T(1024)(128)(4,1)S(1)}, s32[]{:S(2)}) async-start(s8[6291456]{0:T(1024)(128)(4,1)} %bitcast.128), calls=%async_computation.6 | async-start | bytes 8388608
  172.1 11.7 %slice-start.5 = ((s8[6291456]{0:T(1024)(128)(4,1)}), s8[2097152]{0:T(1024)(128)(4,1)S(1)}, s32[]{:S(2)}) async-start(s8[6291456]{0:T(1024)(128)(4,1)} %bitcast.128), calls=%async_computation.7 | async-start | bytes 4194304
  187.4 7.2 %collective-permute-start.12 = (bf16[1024,2048]{1,0:T(8,128)(2,1)S(1)}, bf16[1024,2048]{1,0:T(8,128)(2,1)S(1)}, u32[]{:S(2)}, u32[]{:S(2)}) collective-permute-start(bf16[1024,2048]{1,0:T(8,128)(2,1)S(1)} %convolution_convert_fusion), channel_id=1, source_target_pairs={{0,1},{1,0},{2,3},{3,2},{4,5},{5,4},{6,7},{7,6},{8,9},{9,8},{10,11... | collective-permute-start | bytes 12582920 | tf_op jit(solution)/shard_map/ppermute | solution.py:117
  199.7 57.5 %all-to-all-start.1 = ((bf16[128,8,2048]{2,1,0:T(8,128)(2,1)}), bf16[128,8,2048]{2,1,0:T(8,128)(2,1)}, u32[]{:S(2)}, u32[]{:S(2)}) async-start(bf16[128,8,2048]{2,1,0:T(8,128)(2,1)} %fusion.3), calls=%async_computation.1 | async-start | bytes 8388608 | tf_op jit(solution)/shard_map/all_to_all | solution.py:216
  (2 other events, 8.7 us)

commit v2 on v1

v2 whole, which is shorter than its diff:
```python
import jax
import jax.numpy as jnp
from jax import lax
from jax.experimental import pallas as pl
from jax.experimental.pallas import tpu as pltpu
from jax.sharding import Mesh
from jax.sharding import PartitionSpec as P

HEAD = 128
TOP = 3
CAP = 8
AXES = ("group", "y", "core")
LOG2E = 1.4426950408889634
ORDER = (2, 1, 3, 0)


def attention_kernel(where_ref, q_ref, k_ref, v_ref, o_ref):
    rows = q_ref.shape[1]
    heads = q_ref.shape[2] // HEAD
    place = where_ref[pl.program_id(0)]
    core = where_ref[4]
    scale = HEAD ** (-0.5) * LOG2E
    for block in range(4):

        @pl.when(place == block)
        def _():
            columns = 256 * (block + 1)
            keys = k_ref[0:columns, :]
            values = v_ref[0:columns, :]
            row = lax.broadcasted_iota(jnp.int32, (2 * rows, 256), 0) % rows
            column = lax.broadcasted_iota(jnp.int32, (2 * rows, 256), 1)
            allowed = column <= row + core * rows

            for index in range(heads // 2):
                start = index * 2 * HEAD
                both = q_ref[0, :, start : start + 2 * HEAD]
                q = jnp.concatenate([both[:, :HEAD], both[:, HEAD:]], axis=0)
                scores = lax.dot_general(
                    q, keys, (((1,), (1,)), ((), ())), preferred_element_type=jnp.float32
                )
                last = jnp.where(allowed, scores[:, columns - 256 :], -1e30)
                if block:
                    scores = jnp.concatenate([scores[:, : columns - 256], last], axis=1)
                else:
                    scores = last
                largest = jnp.max(scores, axis=1, keepdims=True)
                weights = jnp.exp2((scores - largest) * scale).astype(jnp.bfloat16)
                context = jnp.dot(weights, values, preferred_element_type=jnp.float32)
                context = (context[:, :HEAD] / context[:, HEAD:]).astype(jnp.bfloat16)
                o_ref[0, :, start : start + 2 * HEAD] = jnp.concatenate(
                    [context[:rows], context[rows:]], axis=1
                )


def attention(where, queries, keys, values):
    ring, rows, width = queries.shape
    return pl.pallas_call(
        attention_kernel,
        out_shape=jax.ShapeDtypeStruct((ring, rows, width), jnp.bfloat16),
        grid_spec=pltpu.PrefetchScalarGridSpec(
            num_scalar_prefetch=1,
            grid=(ring,),
            in_specs=[
                pl.BlockSpec((1, rows, width), lambda i, w: (i, 0, 0)),
                pl.BlockSpec(keys.shape, lambda i, w: (0, 0)),
                pl.BlockSpec(values.shape, lambda i, w: (0, 0)),
            ],
            out_specs=pl.BlockSpec((1, rows, width), lambda i, w: (i, 0, 0)),
        ),
        compiler_params=pltpu.CompilerParams(vmem_limit_bytes=20 * 1024 * 1024),
        cost_estimate=pl.CostEstimate(
            flops=ring * 8 * rows * 2560 * HEAD, bytes_accessed=ring << 20, transcendentals=ring * 2 * rows * 2560
        ),
    )(where, queries, keys, values)


def fdot(a, b):
    return jnp.dot(a, b, preferred_element_type=jnp.float32)


def project_kernel(context_ref, own_ref, other_ref, o_ref):
    half = own_ref.shape[0]
    result = jnp.dot(
        context_ref[:, :half], own_ref[...], preferred_element_type=jnp.float32
    ) + jnp.dot(context_ref[:, half:], other_ref[...], preferred_element_type=jnp.float32)
    o_ref[...] = result.astype(o_ref.dtype)


def project(context, weight_own, weight_other, dtype, tile=1024):
    ring, rows, depth = context.shape
    context = context.reshape(ring * rows, depth)
    half, width = weight_own.shape
    return pl.pallas_call(
        project_kernel,
        out_shape=jax.ShapeDtypeStruct((ring * rows, width), dtype),
        grid=(width // tile,),
        in_specs=[
            pl.BlockSpec((ring * rows, depth), lambda j: (0, 0)),
            pl.BlockSpec((half, tile), lambda j: (0, j)),
            pl.BlockSpec((half, tile), lambda j: (0, j)),
        ],
        out_specs=pl.BlockSpec((ring * rows, tile), lambda j: (0, j)),
        compiler_params=pltpu.CompilerParams(vmem_limit_bytes=16 * 1024 * 1024),
        cost_estimate=pl.CostEstimate(
            flops=2 * ring * rows * depth * width, bytes_accessed=2 * depth * width, transcendentals=0
        ),
    )(context, weight_own, weight_other)


def gated_kernel(x_ref, gate_ref, up_ref, o_ref):
    x = x_ref[...]
    gate = jnp.dot(x, gate_ref[0], preferred_element_type=jnp.float32)
    upward = jnp.dot(x, up_ref[0], preferred_element_type=jnp.float32)
    o_ref[...] = (gate / (1.0 + jnp.exp(-gate)) * upward).astype(jnp.bfloat16)


def gated(x, w_gate, w_up, tile=256):
    rows, depth = x.shape
    hidden = w_gate.shape[2]
    return pl.pallas_call(
        gated_kernel,
        out_shape=jax.ShapeDtypeStruct((rows, hidden), jnp.bfloat16),
        grid=(hidden // tile,),
        in_specs=[
            pl.BlockSpec((rows, depth), lambda j: (0, 0)),
            pl.BlockSpec((1, depth, tile), lambda j: (0, 0, j)),
            pl.BlockSpec((1, depth, tile), lambda j: (0, 0, j)),
        ],
        out_specs=pl.BlockSpec((rows, tile), lambda j: (0, j)),
        compiler_params=pltpu.CompilerParams(vmem_limit_bytes=24 * 1024 * 1024),
        cost_estimate=pl.CostEstimate(
            flops=4 * rows * depth * hidden,
            bytes_accessed=4 * depth * hidden + 2 * rows * depth,
            transcendentals=rows * hidden,
        ),
    )(x, w_gate, w_up)


def down_kernel(a_ref, w_ref, o_ref):
    o_ref[...] = jnp.dot(a_ref[...], w_ref[0], preferred_element_type=jnp.float32).astype(
        jnp.bfloat16
    )


def down_add_kernel(a_ref, w_ref, other_ref, *refs):
    part = jnp.dot(a_ref[...], w_ref[0], preferred_element_type=jnp.float32)
    part = part.astype(jnp.bfloat16).astype(jnp.float32)
    refs[-1][...] = (part + other_ref[...].astype(jnp.float32)).astype(jnp.bfloat16)


def down(activation, w_down, side, added=None, into=None, tile=1024):
    rows, hidden = activation.shape
    width = w_down.shape[2]
    steps = width // 2 // tile
    first = side * steps
    in_specs = [
        pl.BlockSpec((rows, hidden), lambda j: (0, 0)),
        pl.BlockSpec((1, hidden, tile), lambda j: (0, 0, j + first)),
    ]
    args = [activation, w_down]
    aliases = {}
    if added is None:
        kernel, out_width, place = down_kernel, width // 2, 0
    else:
        kernel, out_width, place = down_add_kernel, width, first
        in_specs.append(pl.BlockSpec((rows, tile), lambda j: (0, j)))
        args.append(added)
        if into is not None:
            in_specs.append(pl.BlockSpec(memory_space=pl.ANY))
            args.append(into)
            aliases = {3: 0}
    return pl.pallas_call(
        kernel,
        out_shape=jax.ShapeDtypeStruct((rows, out_width), jnp.bfloat16),
        grid=(steps,),
        in_specs=in_specs,
        out_specs=pl.BlockSpec((rows, tile), lambda j: (0, j + place)),
        input_output_aliases=aliases,
        compiler_params=pltpu.CompilerParams(vmem_limit_bytes=16 * 1024 * 1024),
        cost_estimate=pl.CostEstimate(
            flops=rows * hidden * width,
            bytes_accessed=hidden * width + rows * width,
            transcendentals=0,
        ),
    )(*args)


def local(
    queries,
    rotated_key_rows,
    value_row_matrix,
    out_weight,
    residual,
    norm_gain,
    expert_ids,
    gate_weights,
    w_gate,
    w_up,
    w_down,
):
    bf16, f32 = jnp.bfloat16, jnp.float32
    rows = queries.shape[0]
    width = residual.shape[1]
    ring = lax.axis_size("y")
    experts = lax.axis_size("group") * ring
    y, core = lax.axis_index("y"), lax.axis_index("core")
    other = 1 - core
    chip_width = queries.shape[1] // ring
    half_width = chip_width // 2
    half = width // 2

    def along(value, step):
        return lax.ppermute(value, "y", [(i, (i + step) % ring) for i in range(ring)])

    def swap(value):
        return lax.ppermute(value, "core", [(0, 1), (1, 0)])

    def columns(value, start, size):
        return lax.dynamic_slice_in_dim(value, start, size, axis=1)

    weight_other = swap(out_weight)

    def outgoing(step):
        to = (y + step) % ring
        key_head = to * rotated_key_rows.shape[1] // HEAD // ring * HEAD
        return jnp.concatenate(
            [
                columns(queries, to * chip_width + core * half_width, half_width),
                columns(queries, to * chip_width + other * half_width, half_width),
                columns(rotated_key_rows, key_head, HEAD),
                columns(value_row_matrix, key_head, HEAD),
            ],
            axis=1,
        )

    arrived = {step: along(outgoing(step), step) for step in (2, 1, 3)}
    arrived[0] = outgoing(0)
    blocks = [arrived[(-s) % ring] for s in ORDER]
    key_values = jnp.stack([arrived[(-step) % ring][:, chip_width:] for step in range(ring)])
    key_values_other = swap(key_values)
    gathered = jnp.where(
        core == 0,
        jnp.stack([key_values, key_values_other], axis=1),
        jnp.stack([key_values_other, key_values], axis=1),
    )
    gathered = jnp.stack(
        [
            lax.dynamic_index_in_dim(gathered, (place - y) % ring, axis=0, keepdims=False)
            for place in range(ring)
        ]
    )
    gathered = gathered.reshape(ring * 2 * rows, 2 * HEAD)
    keys = gathered[:, :HEAD]
    values = jnp.concatenate([gathered[:, HEAD:], jnp.ones_like(keys)], axis=1)

    def attend(first, last):
        places = [(y + step) % ring for step in ORDER[first:last]]
        places = places + [places[0]] * (ring - len(places)) + [core]
        context = jnp.stack([block[:, :chip_width] for block in blocks[first:last]])
        return jnp.stack(places).astype(jnp.int32), context

    where, block = attend(0, 1)
    opposite = project(attention(where, block, keys, values), out_weight, weight_other, bf16)
    from_left = along(opposite[:, :half], 1)
    from_right = along(opposite[:, half:], -1)
    where, block = attend(1, 3)
    block, opposite = lax.optimization_barrier((block, opposite))
    partial = project(attention(where, block, keys, values), out_weight, weight_other, bf16)
    right, left = partial[:rows], partial[rows:]
    right_plain = along(right[:, half:], 1)
    left_plain = along(left[:, :half], -1)
    right_sum = along((right[:, :half].astype(f32) + from_left.astype(f32)).astype(bf16), 1)
    left_sum = along((left[:, half:].astype(f32) + from_right.astype(f32)).astype(bf16), -1)
    where, block = attend(3, 4)
    block, partial = lax.optimization_barrier((block, partial))
    own = project(attention(where, block, keys, values), out_weight, weight_other, f32)
    hidden = residual.astype(f32) + own
    hidden = hidden + jnp.concatenate(
        [
            right_sum.astype(f32) + left_plain.astype(f32),
            right_plain.astype(f32) + left_sum.astype(f32),
        ],
        axis=1,
    )

    mean_square = jnp.mean(hidden * hidden, axis=-1, keepdims=True)
    moe_input = (hidden * lax.rsqrt(mean_square + 1e-06) * norm_gain).astype(bf16)

    flat_ids = expert_ids.reshape(-1)
    one_hot = (flat_ids[:, None] == jnp.arange(experts, dtype=jnp.int32)[None, :]).astype(jnp.int32)
    earlier = jnp.cumsum(one_hot, axis=0) - one_hot
    rank_within = jnp.sum(earlier * one_hot, axis=1)
    slot_index = (flat_ids * CAP + rank_within).reshape(rows, TOP)
    slot_rows = jnp.arange(experts * CAP, dtype=jnp.int32)
    hit = [slot_rows[:, None] == slot_index[:, k][None, :] for k in range(TOP)]
    selector = (hit[0] | hit[1] | hit[2]).astype(bf16)
    spread = sum(
        jnp.where(slot_rows[None, :] == slot_index[:, k][:, None], gate_weights[:, k][:, None], 0.0)
        for k in range(TOP)
    )
    spread_high = spread.astype(bf16)
    spread_low = (spread - spread_high.astype(f32)).astype(bf16)

    slots = fdot(selector, moe_input).astype(bf16).reshape(experts, CAP, width)
    mine = lax.all_to_all(slots, ("group", "y"), split_axis=0, concat_axis=0, tiled=True)
    mine = mine.reshape(experts * CAP, width)
    theirs = swap(mine)

    active_mine = gated(mine, w_gate, w_up)
    theirs, active_mine = lax.optimization_barrier((theirs, active_mine))
    active_theirs = gated(theirs, w_gate, w_up)
    back = [swap(down(active_theirs, w_down, side)) for side in (0, 1)]
    expert_out = down(active_mine, w_down, 0, back[0])
    expert_out = down(active_mine, w_down, 1, back[1], expert_out)
    returned = lax.all_to_all(
        expert_out.reshape(experts, CAP, width),
        ("group", "y"),
        split_axis=0,
        concat_axis=0,
        tiled=True,
    ).reshape(experts * CAP, width)
    routed = fdot(spread_high, returned) + fdot(spread_low, returned)
    return (hidden + routed).astype(bf16)


def solution(mesh):
    devices = mesh.devices
    mesh = Mesh(devices.reshape(devices.shape[0], devices.shape[1] // 2, 2), AXES)
    wide = P(AXES, None)
    deep = P(AXES, None, None)
    return jax.shard_map(
        local,
        mesh=mesh,
        in_specs=(
            wide,
            wide,
            wide,
            P(("y", "core"), None),
            wide,
            P(),
            wide,
            wide,
            deep,
            deep,
            deep,
        ),
        out_specs=wide,
        check_vma=False,
    )
```

time: 266 us -> 237 us (0.89)
  matrix products: 65.1 us -> 8.47 us
  Pallas kernels: 9.64 us -> 45.3 us
  waiting for transfers between devices: 94.7 us -> 84.2 us
  blocking collectives: 62.6 us -> 57.5 us
  local copies, waits for them, and re-layouts: 5.43 us -> 8.4 us
  starting transfers between devices: 22.8 us -> 25.5 us
    dot_general x15 -> x3, matrix products: 58.1 us -> 8.47 us  [fdot(): return jnp.dot(a, b, preferred_element_type=jnp.float32)]
    pallas_call x0 -> x9, Pallas kernels: none -> 38.9 us  [the longest x2 15.9 us: gated(): pl.pallas_call(gated_kernel, out_shape=jax.ShapeDtypeStruct((rows, hidden...]
    ppermute x13 -> x14, waiting for transfers between devices: 42.7 us -> 30.2 us  [the longest x9 27.4 us: along(): lax.ppermute(value, 'y', [(i, (i + step) % ring) for i in range(ring)])]
    dot_general x2 -> x0, matrix products: 6.96 us -> none  [gather_back(): lax.dot_general(weights, returned, (((0,), (0,)), ((), ())), preferred_el...]
    all_to_all x1, blocking collectives: 62.6 us -> 57.5 us  [local(): lax.all_to_all(slots, ('group', 'y'), split_axis=0, concat_axis=0, tiled=...]
    unnamed x25 -> x27, local copies, waits for them, and re-layouts: 0.18 us -> 4.51 us
    pallas_call x1 -> x3, Pallas kernels: 9.64 us -> 6.39 us  [attention(): pl.pallas_call(attention_kernel, out_shape=jax.ShapeDtypeStruct((ring, ro...]
    ppermute x13 -> x14, starting transfers between devices: 17.6 us -> 19.3 us  [the longest x9 11.6 us: along(): lax.ppermute(value, 'y', [(i, (i + step) % ring) for i in range(ring)])]
  transfers between devices with their start and end apart: 14 -> 15, of which waited for: 9 -> 9; matrix products, arithmetic and copies ran while one was open for 13% -> 3% of each run, Pallas kernels for 4% -> 12%
where the time goes in v2:
time: 237 us; the launch traced here: 234 us
  waiting for transfers between devices  84.2 us (36%)
  blocking collectives  57.5 us (24%)
  Pallas kernels  45.3 us (19%)
  starting transfers between devices  25.5 us (11%)
  matrix products  8.47 us (4%)
  local copies, waits for them, and re-layouts  8.4 us (4%)
  other arithmetic  4.35 us (2%)
    all_to_all x1, blocking collectives, local(): lax.all_to_all(slots, ('group', 'y'), split_axis=0, concat_axis=0, tiled=...  57.5 us
    all_to_all x1, waiting for transfers between devices, local(): lax.all_to_all(expert_out.reshape(experts, CAP, width), ('group', 'y'), s...  54 us
    ppermute x9, waiting for transfers between devices, along(): lax.ppermute(value, 'y', [(i, (i + step) % ring) for i in range(ring)])  27.4 us
    pallas_call x2, Pallas kernels, gated(): pl.pallas_call(gated_kernel, out_shape=jax.ShapeDtypeStruct((rows, hidden...  15.9 us
    pallas_call x3, Pallas kernels, project(): pl.pallas_call(project_kernel, out_shape=jax.ShapeDtypeStruct((ring * row...  13.3 us
    ppermute x9, starting transfers between devices, along(): lax.ppermute(value, 'y', [(i, (i + step) % ring) for i in range(ring)])  11.6 us
    pallas_call x4, Pallas kernels, down(): pl.pallas_call(kernel, out_shape=jax.ShapeDtypeStruct((rows, out_width),...  9.71 us
    dot_general x3, matrix products, fdot(): return jnp.dot(a, b, preferred_element_type=jnp.float32)  8.47 us
  transfers between devices with their start and end apart: 15, of which 9 were waited for; matrix products, arithmetic and copies ran while one was open for 3% of the time, Pallas kernels for 12%

profile of v2, /device:TPU:1, one launch (start us, length us, event | category | flops | bytes accessed | tf_op | source)
XLA Modules:
  0.0 234.2 jit_solution(3808994181625596155)
XLA Ops:
  3.8 2.9 %collective-permute-start = (bf16[128,1280]{1,0:T(8,128)(2,1)S(1)}, bf16[128,1280]{1,0:T(8,128)(2,1)S(1)}, u32[]{:S(2)}, u32[]{:S(2)}) collective-permute-start(bf16[128,1280]{1,0:T(8,128)(2,1)S(1)} %pad_maximum_fusion.2), channel_id=1, source_target_pairs={{0,6},{2,0},{4,2},{6,4},{1,7},{3,1},{5,3},{7,5},{8,14},{10,8},{12,... | collective-permute-start | bytes 983048 | tf_op jit(solution)/shard_map/ppermute | solution.py:213
  10.8 9.8 %collective-permute-done = bf16[128,1280]{1,0:T(8,128)(2,1)S(1)} collective-permute-done((bf16[128,1280]{1,0:T(8,128)(2,1)S(1)}, bf16[128,1280]{1,0:T(8,128)(2,1)S(1)}, u32[]{:S(2)}, u32[]{:S(2)}) %collective-permute-start) | collective-permute-done | bytes 327712 | tf_op jit(solution)/shard_map/ppermute | solution.py:213
  20.7 3.3 %collective-permute-done.1 = bf16[128,1280]{1,0:T(8,128)(2,1)S(1)} collective-permute-done((bf16[128,1280]{1,0:T(8,128)(2,1)S(1)}, bf16[128,1280]{1,0:T(8,128)(2,1)S(1)}, u32[]{:S(2)}, u32[]{:S(2)}) %collective-permute-start.1) | collective-permute-done | bytes 327712 | tf_op jit(solution)/shard_map/ppermute | solution.py:213
  28.9 4.2 %shard_map.110 = bf16[128,4096]{1,0:T(8,128)(2,1)S(1)} custom-call(bf16[128,1024]{1,0:T(8,128)(2,1)S(1)} %bitcast.74, bf16[512,4096]{1,0:T(8,128)(2,1)S(1)} %copy-done.1, bf16[512,4096]{1,0:T(8,128)(2,1)} %collective-permute-done.4.other_ref), custom_call_target="tpu_custom_call" | custom-call | flops 1073741824 | bytes 8388608 | tf_op jit(solution)/shard_map/pallas_call | solution.py:93
  33.2 2.7 %collective-permute-start.9 = (bf16[128,2048]{1,0:T(8,128)(2,1)S(1)}, bf16[128,2048]{1,0:T(8,128)(2,1)S(1)}, u32[]{:S(2)}, u32[]{:S(2)}) collective-permute-start(bf16[128,2048]{1,0:T(8,128)(2,1)S(1)} %get-tuple-element.28), channel_id=1, source_target_pairs={{0,6},{2,0},{4,2},{6,4},{1,7},{3,1},{5,3},{7,5},{8,14},{10,8},{12,... | collective-permute-start | bytes 1572872 | tf_op jit(solution)/shard_map/ppermute | solution.py:213
  35.9 3.3 %shard_map.111 = bf16[2,128,1024]{2,1,0:T(8,128)(2,1)S(1)} custom-call(s32[5]{0:T(128)S(1)} %stack.91.where_ref, bf16[2,128,1024]{2,1,0:T(8,128)(2,1)S(1)} %pad_maximum_fusion.q_ref, bf16[1024,128]{1,0:T(8,128)(2,1)S(1)} %get-tuple-element.30.k_ref, bf16[1024,256]{1,0:T(8,128)(2,1)S(1)} %concatenate.27.v_ref), custom_call_target="tpu_custom_call" | custom-call | flops 671088640 | bytes 2097152 | tf_op jit(solution)/shard_map/pallas_call | solution.py:57
  39.2 5.0 %shard_map.112 = bf16[256,4096]{1,0:T(8,128)(2,1)S(1)} custom-call(bf16[256,1024]{1,0:T(8,128)(2,1)S(1)} %bitcast.76, bf16[512,4096]{1,0:T(8,128)(2,1)S(1)} %copy-done.1, bf16[512,4096]{1,0:T(8,128)(2,1)} %collective-permute-done.4.other_ref), custom_call_target="tpu_custom_call" | custom-call | flops 2147483648 | bytes 8388608 | tf_op jit(solution)/shard_map/pallas_call | solution.py:93
  44.3 3.2 %collective-permute-done.5 = bf16[128,2048]{1,0:T(8,128)(2,1)S(1)} collective-permute-done((bf16[128,2048]{1,0:T(8,128)(2,1)S(1)}, bf16[128,2048]{1,0:T(8,128)(2,1)S(1)}, u32[]{:S(2)}, u32[]{:S(2)}) %collective-permute-start.5) | collective-permute-done | bytes 524320 | tf_op jit(solution)/shard_map/ppermute | solution.py:213
  50.9 3.2 %collective-permute-start.10 = (bf16[128,2048]{1,0:T(8,128)(2,1)S(1)}, bf16[128,2048]{1,0:T(8,128)(2,1)S(1)}, u32[]{:S(2)}, u32[]{:S(2)}) collective-permute-start(bf16[128,2048]{1,0:T(8,128)(2,1)S(1)} %get-tuple-element.16), channel_id=1, source_target_pairs={{0,6},{2,0},{4,2},{6,4},{1,7},{3,1},{5,3},{7,5},{8,14},{10,8},{12,... | collective-permute-start | bytes 1572872 | tf_op jit(solution)/shard_map/ppermute | solution.py:213
  54.1 2.2 copy-done.2
  56.3 4.2 %shard_map.114 = f32[128,4096]{1,0:T(8,128)S(1)} custom-call(bf16[128,1024]{1,0:T(8,128)(2,1)S(1)} %bitcast.75, bf16[512,4096]{1,0:T(8,128)(2,1)S(1)} %copy-done.2, bf16[512,4096]{1,0:T(8,128)(2,1)} %collective-permute-done.4.other_ref), custom_call_target="tpu_custom_call" | custom-call | flops 1073741824 | bytes 8388608 | tf_op jit(solution)/shard_map/pallas_call | solution.py:93
  62.8 10.0 %collective-permute-done.8 = bf16[128,2048]{1,0:T(8,128)(2,1)S(1)} collective-permute-done((bf16[128,2048]{1,0:T(8,128)(2,1)S(1)}, bf16[128,2048]{1,0:T(8,128)(2,1)S(1)}, u32[]{:S(2)}, u32[]{:S(2)}) %collective-permute-start.8) | collective-permute-done | bytes 524320 | tf_op jit(solution)/shard_map/ppermute | solution.py:213
  74.8 57.5 %all_to_all.10 = bf16[64,8,4096]{2,1,0:T(8,128)(2,1)S(1)} all-to-all(bf16[64,8,4096]{2,1,0:T(8,128)(2,1)S(1)} %fusion), channel_id=1, replica_groups=mesh['group'=16,'y'=4,'core'=2] {'group','y'}, dimensions={0} | all-to-all | bytes 8388608 | tf_op jit(solution)/shard_map/all_to_all | solution.py:305
  132.3 4.5 %collective-permute-start.11 = (bf16[512,4096]{1,0:T(8,128)(2,1)S(1)}, bf16[512,4096]{1,0:T(8,128)(2,1)S(1)}, u32[]{:S(2)}, u32[]{:S(2)}) collective-permute-start(bf16[512,4096]{1,0:T(8,128)(2,1)S(1)} %bitcast.72), channel_id=1, source_target_pairs={{0,1},{1,0},{2,3},{3,2},{4,5},{5,4},{6,7},{7,6},{8,9},{9,8},{10,11... | collective-permute-start | bytes 12582920 | tf_op jit(solution)/shard_map/ppermute | solution.py:216
  136.8 7.9 %shard_map.115.a_ref = bf16[512,768]{1,0:T(8,128)(2,1)S(1)} custom-call(bf16[512,4096]{1,0:T(8,128)(2,1)S(1)} %bitcast.73, bf16[1,4096,768]{2,1,0:T(8,128)(2,1)S(1)} %bitcast.78, bf16[1,4096,768]{2,1,0:T(8,128)(2,1)S(1)} %bitcast.80), custom_call_target="tpu_custom_call" | custom-call | flops 6442450944 | bytes 16777216 | tf_op jit(solution)/shard_map/pallas_call | solution.py:120
  144.8 7.9 %shard_map.116.a_ref = bf16[512,768]{1,0:T(8,128)(2,1)S(1)} custom-call(bf16[512,4096]{1,0:T(8,128)(2,1)S(1)} %collective-permute-done.11.x_ref, bf16[1,4096,768]{2,1,0:T(8,128)(2,1)S(1)} %bitcast.78, bf16[1,4096,768]{2,1,0:T(8,128)(2,1)S(1)} %bitcast.80), custom_call_target="tpu_custom_call" | custom-call | flops 6442450944 | bytes 16777216 | tf_op jit(solution)/shard_map/pallas_call | solution.py:120
  152.7 2.3 shard_map.118
  155.2 2.3 shard_map.117
  159.3 2.5 %shard_map.119.refs_0_ = bf16[512,4096]{1,0:T(8,128)(2,1)S(1)} custom-call(bf16[512,768]{1,0:T(8,128)(2,1)S(1)} %shard_map.115.a_ref, bf16[1,768,4096]{2,1,0:T(8,128)(2,1)S(1)} %bitcast.70, bf16[512,2048]{1,0:T(8,128)(2,1)S(1)} %collective-permute-done.13.other_ref), custom_call_target="tpu_custom_call" | custom-call | flops 1610612736 | bytes 5242880 | tf_op jit(solution)/shard_map/pallas_call | solution.py:172
  162.3 2.5 %shard_map.120 = bf16[512,4096]{1,0:T(8,128)(2,1)S(1)} custom-call(bf16[512,768]{1,0:T(8,128)(2,1)S(1)} %shard_map.115.a_ref, bf16[1,768,4096]{2,1,0:T(8,128)(2,1)S(1)} %bitcast.70, bf16[512,2048]{1,0:T(8,128)(2,1)S(1)} %collective-permute-done.12.other_ref, bf16[512,4096]{1,0:T(8,128)(2,1)S(1)} %shard_map.119.refs_0_), custom_call_target="tpu_custom_call", output_to_operand_aliasing={{}: (3, {})} | custom-call | flops 1610612736 | bytes 5242880 | tf_op jit(solution)/shard_map/pallas_call | solution.py:172
  166.9 6.2 %all-to-all-start.1 = ((bf16[64,8,4096]{2,1,0:T(8,128)(2,1)}), bf16[64,8,4096]{2,1,0:T(8,128)(2,1)}, u32[]{:S(2)}, u32[]{:S(2)}) async-start(bf16[64,8,4096]{2,1,0:T(8,128)(2,1)} %bitcast.71), calls=%async_computation.1 | async-start | bytes 8388608 | tf_op jit(solution)/shard_map/all_to_all | solution.py:315
  173.1 54.0 %all-to-all-done.1 = bf16[64,8,4096]{2,1,0:T(8,128)(2,1)} async-done(((bf16[64,8,4096]{2,1,0:T(8,128)(2,1)}), bf16[64,8,4096]{2,1,0:T(8,128)(2,1)}, u32[]{:S(2)}, u32[]{:S(2)}) %all-to-all-start.1) | async-done | bytes 4194336 | tf_op jit(solution)/shard_map/all_to_all | solution.py:315
  227.1 3.0 %fusion.3 = f32[128,4096]{1,0:T(8,128)S(1)} fusion(bf16[64,8,4096]{2,1,0:T(8,128)(2,1)} %all-to-all-done.1, f32[128]{0:T(128)S(1)} %get-tuple-element.46, s32[128]{0:T(128)S(1)} %get-tuple-element.49, f32[128]{0:T(128)S(1)} %get-tuple-element.47, s32[128]{0:T(128)S(1)} %get-tuple-element.50, f32[128]{0:T(128)S(1)} %get-tuple-element.45, ...), kind=kOutput, calls=%fused_computation.5 | convolution fusion | flops 537657344 | bytes 6294528 | tf_op jit(solution)/shard_map/dot_general | solution.py:78
  230.1 4.1 %fusion.2 = bf16[128,4096]{1,0:T(8,128)(2,1)} fusion(f32[128,4096]{1,0:T(8,128)S(1)} %get-tuple-element.14, f32[128,4096]{1,0:T(8,128)S(1)} %fusion.3, bf16[64,8,4096]{2,1,0:T(8,128)(2,1)} %all-to-all-done.1, f32[128]{0:T(128)S(1)} %get-tuple-element.46, s32[128]{0:T(128)S(1)} %get-tuple-element.49, f32[128]{0:T(128)S(1)} %get-tuple-element.47, ...), kind=kOutput, calls=%fused_computation.4 | convolution fusion | flops 539033600 | bytes 9440256 | tf_op jit(solution)/shard_map/dot_general | solution.py:78
  (95 shorter events, 24.9 us)
Async XLA Ops:
  0.0 28.8 %collective-permute-start.4 = (bf16[512,4096]{1,0:T(8,128)(2,1)}, bf16[512,4096]{1,0:T(8,128)(2,1)}, u32[]{:S(2)}, u32[]{:S(2)}) collective-permute-start(bf16[512,4096]{1,0:T(8,128)(2,1)} %own_ref.5), channel_id=1, source_target_pairs={{0,1},{1,0},{2,3},{3,2},{4,5},{5,4},{6,7},{7,6},{8,9},{9,8},{10,11... | collective-permute-start | bytes 12582920 | tf_op jit(solution)/shard_map/ppermute | solution.py:216
  2.3 6.2 %copy-start.5 = (s32[128,3]{0,1:T(4,128)S(1)}, s32[128,3]{0,1:T(4,128)}, u32[]{:S(2)}) copy-start(s32[128,3]{0,1:T(4,128)} %param.17) | copy-start | bytes 4612
  3.8 16.9 %collective-permute-start = (bf16[128,1280]{1,0:T(8,128)(2,1)S(1)}, bf16[128,1280]{1,0:T(8,128)(2,1)S(1)}, u32[]{:S(2)}, u32[]{:S(2)}) collective-permute-start(bf16[128,1280]{1,0:T(8,128)(2,1)S(1)} %pad_maximum_fusion.2), channel_id=1, source_target_pairs={{0,6},{2,0},{4,2},{6,4},{1,7},{3,1},{5,3},{7,5},{8,14},{10,8},{12,... | collective-permute-start | bytes 983048 | tf_op jit(solution)/shard_map/ppermute | solution.py:213
  6.7 17.3 %collective-permute-start.1 = (bf16[128,1280]{1,0:T(8,128)(2,1)S(1)}, bf16[128,1280]{1,0:T(8,128)(2,1)S(1)}, u32[]{:S(2)}, u32[]{:S(2)}) collective-permute-start(bf16[128,1280]{1,0:T(8,128)(2,1)S(1)} %pad_maximum_fusion.3), channel_id=1, source_target_pairs={{0,2},{2,4},{4,6},{6,0},{1,3},{3,5},{5,7},{7,1},{8,10},{10,12},{12... | collective-permute-start | bytes 983048 | tf_op jit(solution)/shard_map/ppermute | solution.py:213
  6.8 17.2 %collective-permute-start.2 = (bf16[128,1280]{1,0:T(8,128)(2,1)S(1)}, bf16[128,1280]{1,0:T(8,128)(2,1)S(1)}, u32[]{:S(2)}, u32[]{:S(2)}) collective-permute-start(bf16[128,1280]{1,0:T(8,128)(2,1)S(1)} %pad_maximum_fusion.4), channel_id=1, source_target_pairs={{0,4},{2,6},{4,0},{6,2},{1,5},{3,7},{5,1},{7,3},{8,12},{10,14},{12... | collective-permute-start | bytes 983048 | tf_op jit(solution)/shard_map/ppermute | solution.py:213
  24.1 2.3 %collective-permute-start.3 = (bf16[4,128,256]{2,1,0:T(8,128)(2,1)S(1)}, bf16[4,128,256]{2,1,0:T(8,128)(2,1)S(1)}, u32[]{:S(2)}, u32[]{:S(2)}) collective-permute-start(bf16[4,128,256]{2,1,0:T(8,128)(2,1)S(1)} %get-tuple-element.36), channel_id=1, source_target_pairs={{0,1},{1,0},{2,3},{3,2},{4,5},{5,4},{6,7},{7,6},{8,9},{9,8},{10,11... | collective-permute-start | bytes 786440 | tf_op jit(solution)/shard_map/ppermute | solution.py:216
  33.1 14.4 %collective-permute-start.5 = (bf16[128,2048]{1,0:T(8,128)(2,1)S(1)}, bf16[128,2048]{1,0:T(8,128)(2,1)S(1)}, u32[]{:S(2)}, u32[]{:S(2)}) collective-permute-start(bf16[128,2048]{1,0:T(8,128)(2,1)S(1)} %get-tuple-element.27), channel_id=1, source_target_pairs={{0,2},{2,4},{4,6},{6,0},{1,3},{3,5},{5,7},{7,1},{8,10},{10,12},{12... | collective-permute-start | bytes 1572872 | tf_op jit(solution)/shard_map/ppermute | solution.py:213
  33.2 14.3 %collective-permute-start.9 = (bf16[128,2048]{1,0:T(8,128)(2,1)S(1)}, bf16[128,2048]{1,0:T(8,128)(2,1)S(1)}, u32[]{:S(2)}, u32[]{:S(2)}) collective-permute-start(bf16[128,2048]{1,0:T(8,128)(2,1)S(1)} %get-tuple-element.28), channel_id=1, source_target_pairs={{0,6},{2,0},{4,2},{6,4},{1,7},{3,1},{5,3},{7,5},{8,14},{10,8},{12,... | collective-permute-start | bytes 1572872 | tf_op jit(solution)/shard_map/ppermute | solution.py:213
  44.2 16.3 %collective-permute-start.7 = (bf16[128,2048]{1,0:T(8,128)(2,1)S(1)}, bf16[128,2048]{1,0:T(8,128)(2,1)S(1)}, u32[]{:S(2)}, u32[]{:S(2)}) collective-permute-start(bf16[128,2048]{1,0:T(8,128)(2,1)S(1)} %get-tuple-element.17), channel_id=1, source_target_pairs={{0,6},{2,0},{4,2},{6,4},{1,7},{3,1},{5,3},{7,5},{8,14},{10,8},{12,... | collective-permute-start | bytes 1572872 | tf_op jit(solution)/shard_map/ppermute | solution.py:213
  48.7 12.9 %collective-permute-start.6 = (bf16[128,2048]{1,0:T(8,128)(2,1)}, bf16[128,2048]{1,0:T(8,128)(2,1)}, u32[]{:S(2)}, u32[]{:S(2)}) collective-permute-start(bf16[128,2048]{1,0:T(8,128)(2,1)} %get-tuple-element.15), channel_id=1, source_target_pairs={{0,2},{2,4},{4,6},{6,0},{1,3},{3,5},{5,7},{7,1},{8,10},{10,12},{12... | collective-permute-start | bytes 1572872 | tf_op jit(solution)/shard_map/ppermute | solution.py:213
  48.8 23.9 %collective-permute-start.8 = (bf16[128,2048]{1,0:T(8,128)(2,1)S(1)}, bf16[128,2048]{1,0:T(8,128)(2,1)S(1)}, u32[]{:S(2)}, u32[]{:S(2)}) collective-permute-start(bf16[128,2048]{1,0:T(8,128)(2,1)S(1)} %get-tuple-element.18), channel_id=1, source_target_pairs={{0,2},{2,4},{4,6},{6,0},{1,3},{3,5},{5,7},{7,1},{8,10},{10,12},{12... | collective-permute-start | bytes 1572872 | tf_op jit(solution)/shard_map/ppermute | solution.py:213
  50.9 21.8 %collective-permute-start.10 = (bf16[128,2048]{1,0:T(8,128)(2,1)S(1)}, bf16[128,2048]{1,0:T(8,128)(2,1)S(1)}, u32[]{:S(2)}, u32[]{:S(2)}) collective-permute-start(bf16[128,2048]{1,0:T(8,128)(2,1)S(1)} %get-tuple-element.16), channel_id=1, source_target_pairs={{0,6},{2,0},{4,2},{6,4},{1,7},{3,1},{5,3},{7,5},{8,14},{10,8},{12,... | collective-permute-start | bytes 1572872 | tf_op jit(solution)/shard_map/ppermute | solution.py:213
  60.5 12.3 %copy-start.3 = (bf16[128,4096]{1,0:T(8,128)(2,1)S(1)}, bf16[128,4096]{1,0:T(8,128)(2,1)}, u32[]{:S(2)}) copy-start(bf16[128,4096]{1,0:T(8,128)(2,1)} %param.15) | copy-start | bytes 3145732
  72.9 63.9 %slice-start.2 = ((s8[6291456]{0:T(1024)(128)(4,1)}), s8[4194304]{0:T(1024)(128)(4,1)S(1)}, s32[]{:S(2)}) async-start(s8[6291456]{0:T(1024)(128)(4,1)} %bitcast.77), calls=%async_computation.4 | async-start | bytes 8388608
  72.9 63.9 %slice-start.4 = ((s8[6291456]{0:T(1024)(128)(4,1)}), s8[4194304]{0:T(1024)(128)(4,1)S(1)}, s32[]{:S(2)}) async-start(s8[6291456]{0:T(1024)(128)(4,1)} %bitcast.79), calls=%async_computation.6 | async-start | bytes 8388608
  73.4 63.3 %slice-start.3 = ((s8[6291456]{0:T(1024)(128)(4,1)}), s8[2097152]{0:T(1024)(128)(4,1)S(1)}, s32[]{:S(2)}) async-start(s8[6291456]{0:T(1024)(128)(4,1)} %bitcast.77), calls=%async_computation.5 | async-start | bytes 4194304
  73.4 63.3 %slice-start.5 = ((s8[6291456]{0:T(1024)(128)(4,1)}), s8[2097152]{0:T(1024)(128)(4,1)S(1)}, s32[]{:S(2)}) async-start(s8[6291456]{0:T(1024)(128)(4,1)} %bitcast.79), calls=%async_computation.7 | async-start | bytes 4194304
  74.8 77.9 %slice-start = ((s8[6291456]{0:T(1024)(128)(4,1)}), s8[4194304]{0:T(1024)(128)(4,1)S(1)}, s32[]{:S(2)}) async-start(s8[6291456]{0:T(1024)(128)(4,1)} %bitcast.69), calls=%async_computation.2 | async-start | bytes 8388608
  132.3 20.5 %slice-start.1 = ((s8[6291456]{0:T(1024)(128)(4,1)}), s8[2097152]{0:T(1024)(128)(4,1)S(1)}, s32[]{:S(2)}) async-start(s8[6291456]{0:T(1024)(128)(4,1)} %bitcast.69), calls=%async_computation.3 | async-start | bytes 4194304
  132.3 12.5 %collective-permute-start.11 = (bf16[512,4096]{1,0:T(8,128)(2,1)S(1)}, bf16[512,4096]{1,0:T(8,128)(2,1)S(1)}, u32[]{:S(2)}, u32[]{:S(2)}) collective-permute-start(bf16[512,4096]{1,0:T(8,128)(2,1)S(1)} %bitcast.72), channel_id=1, source_target_pairs={{0,1},{1,0},{2,3},{3,2},{4,5},{5,4},{6,7},{7,6},{8,9},{9,8},{10,11... | collective-permute-start | bytes 12582920 | tf_op jit(solution)/shard_map/ppermute | solution.py:216
  155.1 4.2 %collective-permute-start.13 = (bf16[512,2048]{1,0:T(8,128)(2,1)S(1)}, bf16[512,2048]{1,0:T(8,128)(2,1)S(1)}, u32[]{:S(2)}, u32[]{:S(2)}) collective-permute-start(bf16[512,2048]{1,0:T(8,128)(2,1)S(1)} %shard_map.118), channel_id=1, source_target_pairs={{0,1},{1,0},{2,3},{3,2},{4,5},{5,4},{6,7},{7,6},{8,9},{9,8},{10,11... | collective-permute-start | bytes 6291464 | tf_op jit(solution)/shard_map/ppermute | solution.py:216
  157.5 4.8 %collective-permute-start.12 = (bf16[512,2048]{1,0:T(8,128)(2,1)S(1)}, bf16[512,2048]{1,0:T(8,128)(2,1)S(1)}, u32[]{:S(2)}, u32[]{:S(2)}) collective-permute-start(bf16[512,2048]{1,0:T(8,128)(2,1)S(1)} %shard_map.117), channel_id=1, source_target_pairs={{0,1},{1,0},{2,3},{3,2},{4,5},{5,4},{6,7},{7,6},{8,9},{9,8},{10,11... | collective-permute-start | bytes 6291464 | tf_op jit(solution)/shard_map/ppermute | solution.py:216
  166.9 6.2 %copy-start.6 = (f32[128,3]{0,1:T(4,128)S(1)}, f32[128,3]{0,1:T(4,128)}, u32[]{:S(2)}) copy-start(f32[128,3]{0,1:T(4,128)} %param.18) | copy-start | bytes 4612
  166.9 60.2 %all-to-all-start.1 = ((bf16[64,8,4096]{2,1,0:T(8,128)(2,1)}), bf16[64,8,4096]{2,1,0:T(8,128)(2,1)}, u32[]{:S(2)}, u32[]{:S(2)}) async-start(bf16[64,8,4096]{2,1,0:T(8,128)(2,1)} %bitcast.71), calls=%async_computation.1 | async-start | bytes 8388608 | tf_op jit(solution)/shard_map/all_to_all | solution.py:315
  (4 other events, 7.1 us)
